TPU v7x, 128 devices: a whole 4x4x4 slice. The times are simulated.
128 devices in a mesh: dp: 16 (over y, z), lib: 8 (over x, core).
Axes of the slice: x: 4, y: 4, z: 4, core: 2. Of those that a mesh axis runs over, the one named last changes fastest.
Arguments:
- hidden_in: bfloat16 [65536, 1024], P(('dp', 'lib')), may hold values from -40 to 40
- cotangent: bfloat16 [65536, 1024], P(('dp', 'lib')), may hold values from -1 to 1
- gains: float32 [1, 1024], replicated, may hold values from 0.1 to 1.9
- weights: bfloat16 [1, 4, 1024, 1024], replicated, may hold values from -0.125 to 0.125
- library: bfloat16 [2048, 128, 1024], P(('dp', 'lib')), may hold values from -96 to 96
- neighbours: int32 [1024, 2], P(('dp', 'lib')), may hold values from 0 to 127, as said below
- tile_home: int32 [16, 128], P('dp'), may hold values from 0 to 127, as said below
Outputs:
- hidden_out: bfloat16 [65536, 1024], P(('dp', 'lib'))
- input_grad: bfloat16 [65536, 1024], P(('dp', 'lib'))
- weight_grads: float32 [4096, 1024], P(('dp', 'lib'))
- gain_grads: float32 [1024], P(('dp', 'lib'))
Inputs may be any that keep to these rules, and one draw needn't show every extreme that they name: `tile_home`: row g of each is a permutation of 0 to 127; storage row r of part g is library row g * 128 + r and lies on the device of dp index g and lib index r // 16. `neighbours`: rows are the query blocks of a device in order, 8 per device. Among the 16 ids of one device, at most 4 are stored on any one device of its dp index (owner = tile_home[g, id] // 16); in every draw, each dp index has one owner to which every device of that index sends exactly 4. Ids may repeat.
All inputs are finite; a program needn't handle non-finite values.
Results may differ from a plain program's by a relative error of at most 0.015.
The roundings to bfloat16 on the way count: a program that leaves them out, or rounds other values in their place, can miss the bound.
Values may be sent and summed in bfloat16 or wider, within the bound.
A program may use at most 128 MiB of HBM per device.

v0:
```python
import jax
import jax.numpy as jnp
from jax import lax
from jax.sharding import PartitionSpec as P

HEADS = 16
HD = 64
LAYERS = 1
BLOCK = 64
BLOCKS_SEQ = 4
CAP = 4
SEQ = 256


EPSILON = 1e-06


def matmul_f32(left, right):
    return jnp.dot(left, right, preferred_element_type=jnp.float32)


def batched_local(form, left, right):
    return jnp.einsum(form, left, right, preferred_element_type=jnp.float32)


def shift_up(rows):
    n_seqs = rows.shape[0] // SEQ
    feat_dim = rows.shape[1]
    grouped = rows.reshape(n_seqs, SEQ, feat_dim)
    zero_pad = jnp.zeros((n_seqs, BLOCK - 1, feat_dim), rows.dtype)
    moved_rows = jnp.concatenate([grouped[:, BLOCK - 1 :], zero_pad], axis=1)
    return moved_rows.reshape(n_seqs * BLOCKS_SEQ, BLOCK, feat_dim)


def shift_down(groups):
    feat_dim = groups.shape[-1]
    n_seqs = groups.shape[0] // BLOCKS_SEQ
    grouped = groups.reshape(n_seqs, SEQ, feat_dim)
    zero_pad = jnp.zeros((n_seqs, BLOCK - 1, feat_dim), groups.dtype)
    moved_rows = jnp.concatenate([zero_pad, grouped[:, : SEQ - BLOCK + 1]], axis=1)
    return moved_rows.reshape(n_seqs * SEQ, feat_dim)


def forward_layer(x_rows, gain_row, layer_w, tile_block, batched):
    n_blocks = tile_block.shape[0]
    feat_dim = x_rows.shape[1]
    x_float = x_rows.astype(jnp.float32)
    inv_rms = lax.rsqrt(jnp.mean(x_float * x_float, axis=1, keepdims=True) + EPSILON)
    normed = (x_float * inv_rms * gain_row[None, :]).astype(jnp.bfloat16)
    query = matmul_f32(normed, layer_w[0]).astype(jnp.bfloat16)
    tile_rows = tile_block.reshape(-1, feat_dim)
    key_rows = (
        matmul_f32(tile_rows, layer_w[1]).astype(jnp.bfloat16).reshape(n_blocks, -1, HEADS, HD)
    )
    values = matmul_f32(tile_rows, layer_w[2]).astype(jnp.bfloat16).reshape(n_blocks, -1, HEADS, HD)
    shifted = shift_up(query).reshape(n_blocks, BLOCK, HEADS, HD)
    scores = batched("cqhd,ckhd->chqk", shifted, key_rows) * HD ** (-0.5)
    row_max = jnp.max(scores, axis=-1, keepdims=True)
    exp_scores = jnp.exp(scores - row_max)
    attn_prob = exp_scores / jnp.sum(exp_scores, axis=-1, keepdims=True)
    prob_bf16 = attn_prob.astype(jnp.bfloat16)
    mixed_rows = batched("chqk,ckhd->cqhd", prob_bf16, values).astype(jnp.bfloat16)
    attn_out = shift_down(mixed_rows.reshape(n_blocks, BLOCK, feat_dim))
    layer_out = (x_float + matmul_f32(attn_out, layer_w[3])).astype(jnp.bfloat16)
    saved_state = (
        x_float,
        inv_rms,
        normed,
        shifted,
        key_rows,
        values,
        attn_prob,
        prob_bf16,
        attn_out,
    )
    return (layer_out, saved_state)


def backward_layer(grad_flow, gain_row, layer_w, tile_block, saved_state, batched):
    x_float, inv_rms, normed, shifted, key_rows, values, attn_prob, prob_bf16, attn_out = (
        saved_state
    )
    n_blocks = tile_block.shape[0]
    feat_dim = x_float.shape[1]
    grad_bf16 = grad_flow.astype(jnp.bfloat16)
    d_wo = matmul_f32(attn_out.T, grad_bf16)
    d_attn = matmul_f32(grad_bf16, layer_w[3].T).astype(jnp.bfloat16)
    d_mixed = shift_up(d_attn).reshape(n_blocks, BLOCK, HEADS, HD)
    d_prob = batched("cqhd,ckhd->chqk", d_mixed, values)
    d_values = batched("chqk,cqhd->ckhd", prob_bf16, d_mixed).astype(jnp.bfloat16)
    row_dot = jnp.sum(attn_prob * d_prob, axis=-1, keepdims=True)
    d_scores = (attn_prob * (d_prob - row_dot) * HD ** (-0.5)).astype(jnp.bfloat16)
    d_shifted = batched("chqk,ckhd->cqhd", d_scores, key_rows).astype(jnp.bfloat16)
    d_keys = batched("chqk,cqhd->ckhd", d_scores, shifted).astype(jnp.bfloat16)
    d_query = shift_down(d_shifted.reshape(n_blocks, BLOCK, feat_dim))
    tile_rows = tile_block.reshape(-1, feat_dim)
    d_wq = matmul_f32(normed.T, d_query)
    d_wk = matmul_f32(tile_rows.T, d_keys.reshape(-1, feat_dim))
    d_wv = matmul_f32(tile_rows.T, d_values.reshape(-1, feat_dim))
    d_normed = matmul_f32(d_query, layer_w[0].T)
    d_gain = jnp.sum(d_normed * x_float * inv_rms, axis=0)
    d_hat = d_normed * gain_row[None, :]
    inner = jnp.mean(d_hat * x_float, axis=1, keepdims=True)
    d_x = inv_rms * d_hat - x_float * (inv_rms * inv_rms * inv_rms) * inner
    return (grad_flow + d_x, jnp.stack([d_wq, d_wk, d_wv, d_wo]), d_gain)


def device_step(x_rows, cot_rows, gains, weights, tile_block, batched):
    current = x_rows
    layer_idx = 0
    current, saved_state = forward_layer(
        current, gains[layer_idx], weights[layer_idx], tile_block, batched
    )
    saved_all = [saved_state]
    grad_flow = cot_rows.astype(jnp.float32)
    w_parts = [None] * LAYERS
    g_parts = [None] * LAYERS
    for layer_idx in reversed(range(LAYERS)):
        grad_flow, w_parts[layer_idx], g_parts[layer_idx] = backward_layer(
            grad_flow,
            gains[layer_idx],
            weights[layer_idx],
            tile_block,
            saved_all[layer_idx],
            batched,
        )
    return (current, grad_flow.astype(jnp.bfloat16), jnp.stack(w_parts), jnp.stack(g_parts))


def fetch_tiles(library, neighbours, tile_home):
    n_lib = lax.axis_size("lib")
    lib_dev = library.shape[0]
    home_table = tile_home[0]
    wanted = neighbours.reshape(-1)
    n_requests = wanted.shape[0]
    is_wanted = wanted[:, None] == jnp.arange(home_table.shape[0], dtype=jnp.int32)[None, :]
    stored = jnp.sum(jnp.where(is_wanted, home_table[None, :], 0), axis=1)
    owner_dev = stored // lib_dev
    slot_idx = stored % lib_dev
    req_order = jnp.arange(n_requests, dtype=jnp.int32)
    same_before = (owner_dev[:, None] == owner_dev[None, :]) & (
        req_order[None, :] < req_order[:, None]
    )
    owner_rank = jnp.sum(same_before.astype(jnp.int32), axis=1)
    slot_hit = (owner_dev[:, None, None] == jnp.arange(n_lib, dtype=jnp.int32)[None, :, None]) & (
        owner_rank[:, None, None] == jnp.arange(CAP, dtype=jnp.int32)[None, None, :]
    )
    requested = jnp.sum(jnp.where(slot_hit, slot_idx[:, None, None], 0), axis=0)
    asked_slots = lax.all_to_all(requested, "lib", split_axis=0, concat_axis=0, tiled=True)
    picked = jnp.take(library, asked_slots.reshape(-1), axis=0)
    picked = picked.reshape(asked_slots.shape + library.shape[1:])
    arrived = lax.all_to_all(picked, "lib", split_axis=0, concat_axis=0, tiled=True)
    slot_rows = arrived.reshape((-1,) + library.shape[1:])
    my_tiles = jnp.take(slot_rows, owner_dev * CAP + owner_rank, axis=0)
    return my_tiles.reshape(neighbours.shape[0], -1, library.shape[-1])


def body(hidden_in, cotangent, gains, weights, library, neighbours, tile_home):
    tile_block = fetch_tiles(library, neighbours, tile_home)
    layer_out, grad_out, w_part, g_part = device_step(
        hidden_in, cotangent, gains, weights, tile_block, batched_local
    )
    flat_w = w_part.reshape(-1, w_part.shape[-1])
    flat_g = g_part.reshape(-1)
    w_share, g_share = (
        lax.psum_scatter(flat_w, ("dp", "lib"), scatter_dimension=0, tiled=True),
        lax.psum_scatter(flat_g, ("dp", "lib"), scatter_dimension=0, tiled=True),
    )
    return (layer_out, grad_out, w_share, g_share)


def solution(mesh):
    return jax.shard_map(
        body,
        mesh=mesh,
        in_specs=(
            P(("dp", "lib"), None),
            P(("dp", "lib"), None),
            P(),
            P(),
            P(("dp", "lib"), None, None),
            P(("dp", "lib"), None),
            P("dp", None),
        ),
        out_specs=(
            P(("dp", "lib"), None),
            P(("dp", "lib"), None),
            P(("dp", "lib"), None),
            P(("dp", "lib")),
        ),
        check_vma=False,
    )
```

profile of v0, /device:TPU:0, one launch (start us, length us, event | category | flops | bytes accessed | tf_op | source)
XLA Modules:
  0.0 1070.2 jit_solution(9658144274929613242)
XLA Ops:
  9.3 9.4 all_to_all.14
  20.2 7.1 gather_fusion
  27.3 7.5 broadcast_select_fusion
  34.7 5.1 all-to-all-start.1
  45.0 3.5 reshape_reshape.14
  48.4 3.3 copy.69
  51.7 3.2 fusion.54
  57.6 3.7 copy.71
  61.4 73.1 %all-to-all-done.1 = bf16[8,4,128,1024]{3,2,1,0:T(8,128)(2,1)} async-done(((bf16[8,4,128,1024]{3,2,1,0:T(8,128)(2,1)}), bf16[8,4,128,1024]{3,2,1,0:T(8,128)(2,1)}, u32[]{:S(2)}, u32[]{:S(2)}) %all-to-all-start.1) | async-done | bytes 8388640 | tf_op jit(solution)/shard_map/all_to_all | solution.py:152
  134.4 6.2 gather_fusion.1
  143.3 9.1 convolution_convert_fusion
  152.4 7.6 convolution_convert_fusion.1
  160.0 11.6 %reshape.412 = bf16[8,256,16,64]{3,2,1,0:T(8,128)(2,1)} reshape(bf16[2048,1024]{1,0:T(8,128)(2,1)} %convolution_convert_fusion) | data formatting | bytes 8388608 | tf_op jit(solution)/shard_map/reshape | solution.py:53
  171.6 10.3 copy.62
  181.9 11.6 %reshape.411 = bf16[8,256,16,64]{3,2,1,0:T(8,128)(2,1)} reshape(bf16[2048,1024]{1,0:T(8,128)(2,1)} %convolution_convert_fusion.1) | data formatting | bytes 8388608 | tf_op jit(solution)/shard_map/reshape | solution.py:55
  193.5 10.5 copy.63
  204.0 6.7 fusion.72
  210.7 8.5 fusion.71
  219.2 58.1 %convert_bitcast_fusion.2 = bf16[8,64,16,64]{1,3,2,0:T(8,128)(2,1)} fusion(bf16[8,256,16,64]{1,3,2,0:T(8,128)(2,1)} %copy.62, f32[8,16,64,256]{3,2,1,0:T(8,128)} %fusion.72, f32[8,16,64,256]{3,2,1,0:T(8,128)} %get-tuple-element.11, f32[8,16,64]{2,1,0:T(8,128)S(1)} %get-tuple-element.10), kind=kOutput, calls=%fused_computation.52 | convolution fusion | flops 283648256 | bytes 22052864 | tf_op jit(solution)/shard_map/chqk,ckhd->cqhd/dot_general | solution.py:23
  277.3 57.9 %convert_bitcast_fusion.1 = bf16[8,256,16,64]{1,3,2,0:T(8,128)(2,1)} fusion(bf16[8,64,16,64]{1,3,2,0:T(8,128)(2,1)} %copy.69, f32[8,16,64,256]{3,2,1,0:T(8,128)} %fusion.72, f32[8,16,64,256]{3,2,1,0:T(8,128)} %get-tuple-element.11, f32[8,16,64]{2,1,0:T(8,128)S(1)} %get-tuple-element.10), kind=kOutput, calls=%fused_computation.19 | convolution fusion | flops 285221120 | bytes 22052864 | tf_op jit(solution)/shard_map/chqk,cqhd->ckhd/dot_general | solution.py:23
  335.2 7.5 convert_bitcast_fusion.3
  344.3 2.9 copy.72
  349.4 6.5 convolution_bitcast_fusion.1
  356.0 3.6 copy.64
  363.9 5.1 copy.70
  371.2 6.1 convolution_bitcast_fusion.2
  377.3 3.6 copy.68
  390.7 6.0 pad_maximum_fusion
  396.7 3.6 fusion.27
  400.3 67.2 %all-reduce.4 = f32[1024]{0:T(1024)S(1)} all-reduce(f32[1024]{0:T(1024)S(1)} %get-tuple-element.4), channel_id=3, replica_groups=mesh['dp'=16,'lib'=8] {'dp','lib'}, use_global_device_ids=true, to_apply=%region_10.11.clone | all-reduce | flops 1024 | bytes 8192
  470.9 3.8 fusion.20
  474.8 588.4 %reduce-scatter.2.cloned.1.call-done = f32[32,1024]{1,0:T(8,128)} async-done(((f32[4096,1024]{1,0:T(8,128)}), f32[32,1024]{1,0:T(8,128)}) %reduce-scatter.2.cloned.1.call-update) | async-done | bytes 131088 | tf_op jit(solution)/shard_map/reduce_scatter | solution.py:166
  (71 shorter events, 37.5 us)
Async XLA Ops:
  34.7 5.2 copy-start.1
  34.7 6.1 copy-start.12
  34.7 99.7 %all-to-all-start.1 = ((bf16[8,4,128,1024]{3,2,1,0:T(8,128)(2,1)}), bf16[8,4,128,1024]{3,2,1,0:T(8,128)(2,1)}, u32[]{:S(2)}, u32[]{:S(2)}) async-start(bf16[8,4,128,1024]{3,2,1,0:T(8,128)(2,1)} %broadcast_select_fusion), calls=%async_computation.1 | async-start | bytes 16777216 | tf_op jit(solution)/shard_map/all_to_all | solution.py:152
  39.8 1023.3 %reduce-scatter.2.cloned.1.call-start = ((), (), s32[]{:S(2)}) async-start(), calls=%async_computation.3 | async-start | bytes 16908288 | tf_op jit(solution)/shard_map/reduce_scatter | solution.py:166
  143.3 9.1 copy-start.2
  335.2 7.5 copy-start
  347.3 2.2 copy-start.3
  369.0 2.2 copy-start.4
  384.8 3.2 copy-start.10
  384.8 3.2 copy-start.7
  386.6 1.4 copy-start.8
  386.6 2.7 copy-start.6
  388.0 2.6 copy-start.5
  396.7 71.4 %copy-start.11 = (f32[512]{0:T(512)S(1)}, f32[512]{0:T(512)}, u32[]{:S(2)}) copy-start(f32[512]{0:T(512)} %get-tuple-element.6) | copy-start | bytes 6148
  467.5 3.4 copy-start.9
Sparse Core Ops, SparseCore 0:
  396.8 666.2 reduce-scatter.1
where the time goes:
time: 1080 us; the launch traced here: 1070 us
  waiting for transfers between devices  661 us (61%)
  matrix products  186 us (17%)
  local copies, waits for them, and re-layouts  105 us (10%)
  blocking collectives  76.7 us (7%)
  other arithmetic  21.8 us (2%)
  between operations  14.5 us (1%)
    reduce_scatter x1, waiting for transfers between devices, body(): lax.psum_scatter(flat_w, ('dp', 'lib'), scatter_dimension=0, tiled=True)  588 us
    dot_general x5, matrix products, batched_local(): return jnp.einsum(form, left, right, preferred_element_type=jnp.float32)  132 us
    all_to_all x1, waiting for transfers between devices, fetch_tiles(): lax.all_to_all(picked, 'lib', split_axis=0, concat_axis=0, tiled=True)  73.1 us
    unnamed x1, blocking collectives  67.2 us
    dot_general x10, matrix products, matmul_f32(): return jnp.dot(left, right, preferred_element_type=jnp.float32)  45.5 us
    reshape x2, local copies, waits for them, and re-layouts, forward_layer(): matmul_f32(tile_rows, layer_w[2]).astype(jnp.bfloat16)  22 us
    reshape x2, local copies, waits for them, and re-layouts, forward_layer(): matmul_f32(tile_rows, layer_w[1]).astype(jnp.bfloat16)  21.9 us
  transfers between devices with their start and end apart: 2, of which 2 were waited for; matrix products, arithmetic and copies ran while one was open for 3% of the time, Pallas kernels for 0%

commit v1 on v0

v1 whole, which is shorter than its diff:
```python
import functools

import jax
import jax.numpy as jnp
from jax import lax
from jax.experimental import pallas as pl
from jax.experimental.pallas import tpu as pltpu
from jax.sharding import PartitionSpec as P

HEADS = 16
HD = 64
BLOCK = 64
BLOCKS_SEQ = 4
CAP = 4
SEQ = 256
D = 1024
EPSILON = 1e-06

F32 = jnp.float32
BF16 = jnp.bfloat16
MESH = pl.DeviceIdType.MESH

PARTS = (
    (0, 384, ("x", "y", "z")),
    (384, 384, ("y", "z", "x")),
    (768, 256, ("z", "x", "y")),
)
DIMS = ("y", "z", "x")


def dot(left, right, dims=((1,), (0,))):
    return lax.dot_general(left, right, (dims, ((), ())), preferred_element_type=F32)


def my_coords():
    dp = lax.axis_index("dp")
    lib = lax.axis_index("lib")
    return {
        "y": lax.div(dp, 4),
        "z": lax.rem(dp, 4),
        "x": lax.div(lib, 2),
        "c": lax.rem(lib, 2),
    }


def device_of(at):
    return (at["y"] * 4 + at["z"], at["x"] * 2 + at["c"])


def along(me, axis, step):
    size = 2 if axis == "c" else 4
    return lax.rem(me[axis] + step, size)


def moved(me, axis, step):
    return device_of({**me, axis: along(me, axis, step)})


def stage_shapes(dims, width):
    rest = (4,) * (len(dims) - 1)
    chunk = rest + (32, width)
    half = ((2,) + rest[1:] + (32, width)) if rest else (16, width)
    return [half, half, chunk, chunk]


def part_scratch(part):
    _, width, order = part
    shapes = [pltpu.VMEM((2, 4, 4, 4, 32, width), BF16), pltpu.VMEM((4, 4, 4, 32, width), BF16)]
    dims = list(DIMS)
    n_copies = 1
    for pos, axis in enumerate(order):
        shapes += [pltpu.VMEM(s, BF16) for s in stage_shapes(dims, width)]
        n_copies += 4
        dims.remove(axis)
        if dims:
            shapes.append(pltpu.VMEM((4,) * len(dims) + (32, width), BF16))
    shapes += [pltpu.SemaphoreType.DMA((n_copies,)), pltpu.SemaphoreType.DMA((n_copies,))]
    return shapes


def reduce_part(me, part, bufs, w_out, sent):
    c0, width, order = part
    bufs = list(bufs)
    send_sem, recv_sem = bufs[-2:]
    own, paired = bufs[:2]
    pos = 2
    n = [0]

    def copy(src, dst, device):
        k = n[0]
        n[0] += 1
        cp = pltpu.make_async_remote_copy(
            src_ref=src,
            dst_ref=dst,
            send_sem=send_sem.at[k],
            recv_sem=recv_sem.at[k],
            device_id=device,
            device_id_type=MESH,
        )
        cp.start()
        sent.append(cp)
        return cp

    other = along(me, "c", 1)
    cp = copy(own.at[other], paired, moved(me, "c", 1))
    yield
    cp.wait_recv()

    @pl.loop(0, 16)
    def _(i):
        yi = lax.div(i, 4)
        zi = lax.rem(i, 4)
        total = own[me["c"], yi, zi].astype(F32) + paired[yi, zi].astype(F32)
        paired[yi, zi] = total.astype(BF16)

    data = paired
    dims = list(DIMS)
    for axis in order:
        r1r, r1l, r2r, r2l = bufs[pos : pos + 4]
        pos += 4
        at = dims.index(axis)
        rest = [d for d in dims if d != axis]

        def chunk(step):
            idx = [slice(None)] * len(dims)
            idx[at] = along(me, axis, step)
            return tuple(idx)

        def half(step, h):
            idx = [slice(None)] * (len(dims) + 1)
            idx[at] = along(me, axis, step)
            if rest:
                idx[dims.index(rest[0])] = pl.ds(2 * h, 2)
            else:
                idx[len(dims)] = pl.ds(16 * h, 16)
            return tuple(idx)

        right = moved(me, axis, 1)
        left = moved(me, axis, 3)
        cr = copy(data.at[half(2, 0)], r1r, right)
        cl = copy(data.at[half(2, 1)], r1l, left)
        yield
        cr.wait_recv()
        cl.wait_recv()
        i1 = half(1, 0)
        i3 = half(3, 1)
        data[i1] = (data[i1].astype(F32) + r1r[...].astype(F32)).astype(BF16)
        data[i3] = (data[i3].astype(F32) + r1l[...].astype(F32)).astype(BF16)
        cr = copy(data.at[chunk(1)], r2r, right)
        cl = copy(data.at[chunk(3)], r2l, left)
        yield
        cr.wait_recv()
        cl.wait_recv()
        total = data[chunk(0)].astype(F32) + r2r[...].astype(F32) + r2l[...].astype(F32)
        if rest:
            nxt = bufs[pos]
            pos += 1
            nxt[...] = total.astype(BF16)
            data = nxt
        else:
            w_out[:, c0 : c0 + width] = total
        dims = rest


def reduce_gain(me, slots, send_sem, recv_sem, sent):
    k = 0
    for stage, (axis, size) in enumerate((("c", 2), ("x", 4), ("y", 4), ("z", 4)), 1):
        cps = []
        slots[stage] = slots[0]
        first = k
        for step in range(1, size):
            cp = pltpu.make_async_remote_copy(
                src_ref=slots.at[stage],
                dst_ref=slots.at[5 + k],
                send_sem=send_sem.at[k],
                recv_sem=recv_sem.at[k],
                device_id=moved(me, axis, step),
                device_id_type=MESH,
            )
            cp.start()
            sent.append(cp)
            cps.append(cp)
            k += 1
        yield
        total = slots[stage]
        for i, cp in enumerate(cps):
            cp.wait_recv()
            total = total + slots[5 + first + i]
        slots[0] = total


def shift_up_rows(rows):
    moved_rows = pltpu.roll(rows, SEQ - (BLOCK - 1), 0)
    row = lax.broadcasted_iota(jnp.int32, rows.shape, 0)
    return jnp.where(row < SEQ - BLOCK + 1, moved_rows, 0.0)


def shift_down_rows(rows):
    moved_rows = pltpu.roll(rows, BLOCK - 1, 0)
    row = lax.broadcasted_iota(jnp.int32, rows.shape, 0)
    return jnp.where(row >= BLOCK - 1, moved_rows, 0.0)


def attention_block(b, q_ref, dm_ref, k_ref, v_ref, mixed_ref, dsh_ref):
    hr = lax.broadcasted_iota(jnp.int32, (256, 256), 0) // HD
    hc = lax.broadcasted_iota(jnp.int32, (256, 256), 1) // HD
    same = hr == hc
    hcol = lax.broadcasted_iota(jnp.int32, (64, 256), 1) // HD
    qrows = pl.ds(pl.multiple_of(b * 64, 64), 64)
    krows = pl.ds(pl.multiple_of(b * 256, 256), 256)

    def spread(rows):
        return jnp.where(same, jnp.concatenate([rows] * 4, axis=0), jnp.zeros((), BF16))

    def diag(full):
        out = full[0:64]
        for h in range(1, 4):
            out = jnp.where(hcol == h, full[h * 64 : h * 64 + 64], out)
        return out

    for g in range(4):
        cols = slice(g * 256, g * 256 + 256)
        qbd = spread(q_ref[qrows, cols])
        dobd = spread(dm_ref[qrows, cols])
        keys = k_ref[krows, cols]
        vals = v_ref[krows, cols]
        s = dot(keys, qbd, ((1,), (1,))) * HD ** (-0.5)
        e = jnp.exp(s - jnp.max(s, axis=0, keepdims=True))
        p = e * (1.0 / jnp.sum(e, axis=0, keepdims=True))
        pb = p.astype(BF16)
        mixed_ref[qrows, cols] = diag(dot(pb, vals, ((0,), (0,))))
        dp = dot(vals, dobd, ((1,), (1,)))
        v_ref[krows, cols] = dot(pb, dobd).astype(BF16)
        pdp = p * dp
        rd = jnp.sum(pdp, axis=0, keepdims=True)
        ds = ((pdp - p * rd) * HD ** (-0.5)).astype(BF16)
        dsh_ref[qrows, cols] = diag(dot(ds, keys, ((0,), (0,))))
        k_ref[krows, cols] = dot(ds, qbd).astype(BF16)


def step_kernel(
    x_ref, g_ref, gain_ref, w_ref, t_ref,
    out_ref, grad_ref, wsum_ref, gsum_ref,
    inv_ref, normed_ref, q_ref, dm_ref, k_ref, v_ref, mixed_ref, dsh_ref, dq_ref, attn_ref,
    tt_ref, at_ref, gslots, gsend, grecv, *part_bufs,
):
    me = my_coords()
    barrier = pltpu.get_barrier_semaphore()
    peers = [("c", 1)] + [(a, s) for a in ("x", "y", "z") for s in (1, 2, 3)]
    for axis, step in peers:
        pl.semaphore_signal(barrier, inc=1, device_id=moved(me, axis, step), device_id_type=MESH)
    pl.semaphore_wait(barrier, len(peers))

    @pl.loop(0, 2)
    def _(s):
        rows = pl.ds(pl.multiple_of(s * SEQ, SEQ), SEQ)
        x = x_ref[rows].astype(F32)
        inv = lax.rsqrt(jnp.mean(x * x, axis=1, keepdims=True) + EPSILON)
        inv_ref[rows] = inv
        normed = (x * inv * gain_ref[...]).astype(BF16)
        normed_ref[rows] = normed
        q_ref[rows] = shift_up_rows(dot(normed, w_ref[0])).astype(BF16)
        dm_ref[rows] = shift_up_rows(dot(g_ref[rows], w_ref[3], ((1,), (1,)))).astype(BF16)

    @pl.loop(0, 4)
    def _(i):
        rows = pl.ds(pl.multiple_of(i * 512, 512), 512)
        k_ref[rows] = dot(t_ref[rows], w_ref[1]).astype(BF16)
        v_ref[rows] = dot(t_ref[rows], w_ref[2]).astype(BF16)

    @pl.loop(0, 8)
    def _(b):
        attention_block(b, q_ref, dm_ref, k_ref, v_ref, mixed_ref, dsh_ref)

    @pl.loop(0, 8)
    def _(i):
        rows = pl.ds(pl.multiple_of(i * 256, 256), 256)
        tt_ref[:, rows] = t_ref[rows].T

    gslots[0] = jnp.zeros_like(gslots[0])

    @pl.loop(0, 2)
    def _(s):
        rows = pl.ds(pl.multiple_of(s * SEQ, SEQ), SEQ)
        x = x_ref[rows].astype(F32)
        inv = inv_ref[rows]
        attn = shift_down_rows(mixed_ref[rows]).astype(BF16)
        attn_ref[rows] = attn
        out_ref[rows] = (x + dot(attn, w_ref[3])).astype(BF16)
        dq = shift_down_rows(dsh_ref[rows]).astype(BF16)
        dq_ref[rows] = dq
        dn = dot(dq, w_ref[0], ((1,), (1,)))
        dnx = dn * x * inv
        gslots[0] += jnp.sum(dnx, axis=0, keepdims=True)
        dh = dn * gain_ref[...]
        inner = jnp.mean(dh * x, axis=1, keepdims=True)
        dx = inv * dh - x * (inv * inv * inv) * inner
        grad_ref[rows] = (g_ref[rows].astype(F32) + dx).astype(BF16)
        at_ref[0, :, rows] = normed_ref[rows].T
        at_ref[1, :, rows] = attn.T

    sent = []
    n_each = len(part_bufs) // 3
    flows = [reduce_gain(me, gslots, gsend, grecv, sent)]
    next(flows[0])
    for p, part in enumerate(PARTS):
        c0, width, _ = part
        bufs = part_bufs[p * n_each : (p + 1) * n_each]
        own = bufs[0]
        cols = slice(c0, c0 + width)

        @pl.loop(0, 4)
        def _(z):
            rows = pl.ds(pl.multiple_of(z * 256, 256), 256)
            for j in range(4):
                if j == 0:
                    res = dot(at_ref[0, rows, :], dq_ref[:, cols])
                elif j == 1:
                    res = dot(tt_ref[rows, :], k_ref[:, cols])
                elif j == 2:
                    res = dot(tt_ref[rows, :], v_ref[:, cols])
                else:
                    res = dot(at_ref[1, rows, :], g_ref[:, cols])
                res = res.astype(BF16)
                for xi in range(4):
                    for ci in range(2):
                        r0 = (xi * 2 + ci) * 32
                        own[ci, j, z, xi] = res[r0 : r0 + 32]

        flows.append(reduce_part(me, part, bufs, wsum_ref, sent))
        flows = [f for f in flows if next(f, True) is None]
    while flows:
        flows = [f for f in flows if next(f, True) is None]
    for cp in sent:
        cp.wait_send()
    gsum_ref[...] = gslots[0]


def train_step(hidden, cot, gains, weights, tiles):
    scratch = [
        pltpu.VMEM((512, 1), F32),
        pltpu.VMEM((512, D), BF16),
        pltpu.VMEM((512, D), BF16),
        pltpu.VMEM((512, D), BF16),
        pltpu.VMEM((2048, D), BF16),
        pltpu.VMEM((2048, D), BF16),
        pltpu.VMEM((512, D), F32),
        pltpu.VMEM((512, D), F32),
        pltpu.VMEM((512, D), BF16),
        pltpu.VMEM((512, D), BF16),
        pltpu.VMEM((D, 2048), BF16),
        pltpu.VMEM((2, D, 512), BF16),
        pltpu.VMEM((15, 1, D), F32),
        pltpu.SemaphoreType.DMA((10,)),
        pltpu.SemaphoreType.DMA((10,)),
    ]
    for part in PARTS:
        scratch += part_scratch(part)
    vmem = pl.BlockSpec(memory_space=pltpu.VMEM)
    return pl.pallas_call(
        step_kernel,
        out_shape=(
            jax.ShapeDtypeStruct((512, D), BF16),
            jax.ShapeDtypeStruct((512, D), BF16),
            jax.ShapeDtypeStruct((32, D), F32),
            jax.ShapeDtypeStruct((1, D), F32),
        ),
        in_specs=[vmem] * 5,
        out_specs=(vmem,) * 4,
        scratch_shapes=scratch,
        compiler_params=pltpu.CompilerParams(
            collective_id=1, has_side_effects=True, vmem_limit_bytes=62 * 1024 * 1024
        ),
        name="train_step",
    )(hidden, cot, gains, weights, tiles)


def fetch_tiles(library, neighbours, tile_home):
    n_lib = lax.axis_size("lib")
    lib_dev = library.shape[0]
    home_table = tile_home[0]
    wanted = neighbours.reshape(-1)
    n_requests = wanted.shape[0]
    is_wanted = wanted[:, None] == jnp.arange(home_table.shape[0], dtype=jnp.int32)[None, :]
    stored = jnp.sum(jnp.where(is_wanted, home_table[None, :], 0), axis=1)
    owner_dev = stored // lib_dev
    slot_idx = stored % lib_dev
    req_order = jnp.arange(n_requests, dtype=jnp.int32)
    same_before = (owner_dev[:, None] == owner_dev[None, :]) & (
        req_order[None, :] < req_order[:, None]
    )
    owner_rank = jnp.sum(same_before.astype(jnp.int32), axis=1)
    slot_hit = (owner_dev[:, None, None] == jnp.arange(n_lib, dtype=jnp.int32)[None, :, None]) & (
        owner_rank[:, None, None] == jnp.arange(CAP, dtype=jnp.int32)[None, None, :]
    )
    requested = jnp.sum(jnp.where(slot_hit, slot_idx[:, None, None], 0), axis=0)
    asked_slots = lax.all_to_all(requested, "lib", split_axis=0, concat_axis=0, tiled=True)
    picked = jnp.take(library, asked_slots.reshape(-1), axis=0)
    picked = picked.reshape(asked_slots.shape + library.shape[1:])
    arrived = lax.all_to_all(picked, "lib", split_axis=0, concat_axis=0, tiled=True)
    slot_rows = arrived.reshape((-1,) + library.shape[1:])
    my_tiles = jnp.take(slot_rows, owner_dev * CAP + owner_rank, axis=0)
    return my_tiles.reshape(-1, library.shape[-1])


def body(hidden_in, cotangent, gains, weights, library, neighbours, tile_home):
    tiles = fetch_tiles(library, neighbours, tile_home)
    out, grad, w_share, g_sum = train_step(hidden_in, cotangent, gains, weights[0], tiles)
    index = lax.axis_index("dp") * 8 + lax.axis_index("lib")
    g_share = lax.dynamic_slice(g_sum.reshape(-1), (index * 8,), (8,))
    return (out, grad, w_share, g_share)


def solution(mesh):
    return jax.shard_map(
        body,
        mesh=mesh,
        in_specs=(
            P(("dp", "lib"), None),
            P(("dp", "lib"), None),
            P(),
            P(),
            P(("dp", "lib"), None, None),
            P(("dp", "lib"), None),
            P("dp", None),
        ),
        out_specs=(
            P(("dp", "lib"), None),
            P(("dp", "lib"), None),
            P(("dp", "lib"), None),
            P(("dp", "lib")),
        ),
        check_vma=False,
    )
```

time: 1080 us -> 254 us (0.24)
  waiting for transfers between devices: 661 us -> 94.3 us
  matrix products: 186 us -> 0 us
  Pallas kernels: 0 us -> 109 us
  local copies, waits for them, and re-layouts: 105 us -> 21.4 us
  blocking collectives: 76.7 us -> 9.44 us
  between operations: 14.5 us -> 0.71 us
    reduce_scatter x1 -> x0, waiting for transfers between devices: 588 us -> none  [body(): lax.psum_scatter(flat_w, ('dp', 'lib'), scatter_dimension=0, tiled=True)]
    dot_general x15 -> x0, matrix products: 177 us -> none  [the longest x5 132 us: batched_local(): return jnp.einsum(form, left, right, preferred_element_type=jnp.float32)]
    pallas_call x0 -> x1, Pallas kernels: none -> 109 us  [train_step(): pl.pallas_call(step_kernel, out_shape=(jax.ShapeDtypeStruct((512, D), BF1...]
    unnamed x1 -> x0, blocking collectives: 67.2 us -> none
    reshape x4 -> x0, local copies, waits for them, and re-layouts: 43.9 us -> none  [the longest x2 22 us: forward_layer(): matmul_f32(tile_rows, layer_w[2]).astype(jnp.bfloat16)]
    all_to_all x1, waiting for transfers between devices: 73.1 us -> 94.3 us  [fetch_tiles(): lax.all_to_all(picked, 'lib', split_axis=0, concat_axis=0, tiled=True)]
    another operation x6 -> x0, local copies, waits for them, and re-layouts: 17.5 us -> none  [the longest x2 6.73 us: forward_layer(): shifted = shift_up(query).reshape(n_blocks, BLOCK, HEADS, HD)]
    convert_element_type x4 -> x0, local copies, waits for them, and re-layouts: 15.2 us -> none  [the longest x1 5.06 us: backward_layer(): d_keys = batched('chqk,cqhd->ckhd', d_scores, shifted).astype(jnp.bfloat16)]
  transfers between devices with their start and end apart: 2 -> 1, of which waited for: 2 -> 1; matrix products, arithmetic and copies ran while one was open for 3% -> 0% of each run, Pallas kernels for 0% -> 0%
where the time goes in v1:
time: 254 us; the launch traced here: 253 us
  Pallas kernels  109 us (43%)
  waiting for transfers between devices  94.3 us (37%)
  local copies, waits for them, and re-layouts  21.4 us (8%)
  other arithmetic  13.2 us (5%)
  blocking collectives  9.44 us (4%)
  starting transfers between devices  5.14 us (2%)
    pallas_call x1, Pallas kernels, train_step(): pl.pallas_call(step_kernel, out_shape=(jax.ShapeDtypeStruct((512, D), BF1...  109 us
    all_to_all x1, waiting for transfers between devices, fetch_tiles(): lax.all_to_all(picked, 'lib', split_axis=0, concat_axis=0, tiled=True)  94.3 us
    all_to_all x1, blocking collectives, fetch_tiles(): lax.all_to_all(requested, 'lib', split_axis=0, concat_axis=0, tiled=True)  9.44 us
    select_n x2, other arithmetic, fetch_tiles(): picked = jnp.take(library, asked_slots.reshape(-1), axis=0)  7.47 us
    gather x1, local copies, waits for them, and re-layouts, fetch_tiles(): picked = jnp.take(library, asked_slots.reshape(-1), axis=0)  7.07 us
    gather x1, local copies, waits for them, and re-layouts, fetch_tiles(): my_tiles = jnp.take(slot_rows, owner_dev * CAP + owner_rank, axis=0)  6.17 us
    unnamed x6, local copies, waits for them, and re-layouts  5.94 us
    all_to_all x1, starting transfers between devices, fetch_tiles(): lax.all_to_all(picked, 'lib', split_axis=0, concat_axis=0, tiled=True)  5.14 us
  transfers between devices with their start and end apart: 1, of which 1 were waited for; matrix products, arithmetic and copies ran while one was open for 0% of the time, Pallas kernels for 0%

profile of v1, /device:TPU:0, one launch (start us, length us, event | category | flops | bytes accessed | tf_op | source)
XLA Modules:
  0.0 253.4 jit_solution(3403643664309012437)
XLA Ops:
  0.6 0.8 copy.21
  1.4 0.1 eq.66
  1.5 0.8 select_reduce_fusion.1
  2.3 0.2 convert_reduce_fusion
  2.5 0.1 select_reduce_fusion
  2.7 0.1 copy.22
  2.8 9.4 %all_to_all.14 = s32[8,1,4]{2,1,0:T(1,128)S(1)} all-to-all(s32[8,1,4]{2,1,0:T(1,128)S(1)} %copy.22), channel_id=1, replica_groups=mesh['dp'=16,'lib'=8] {'lib'}, dimensions={0} | all-to-all | bytes 256 | tf_op jit(solution)/shard_map/all_to_all | solution.py:397
  12.2 0.5 broadcast.294
  12.7 0.7 reduce.3
  13.4 0.1 reshape.233
  13.5 0.1 copy.23
  13.6 0.1 copy.24
  13.7 7.1 %gather_fusion = bf16[32,128,1024]{2,1,0:T(8,128)(2,1)} fusion(bf16[16,128,1024]{2,1,0:T(8,128)(2,1)} %param.11, s32[1024]{0:T(1024)S(1)} %pad_clamp_fusion.1), kind=kCustom, calls=%fused_computation | custom fusion | bytes 16777344 | tf_op jit(solution)/shard_map/jit(_take)/gather | solution.py:398
  20.7 7.5 %broadcast_select_fusion = bf16[8,4,128,1024]{3,2,1,0:T(8,128)(2,1)} fusion(bf16[8,4,128,1024]{3,2,1,0:T(8,128)(2,1)} %bitcast.33, pred[8,4]{1,0:T(8,128)(4,1)S(1)} %copy.24), kind=kLoop, calls=%fused_computation.2 | loop fusion | flops 4194304 | bytes 16777248 | tf_op jit(solution)/shard_map/jit(_take)/select_n | solution.py:398
  28.2 5.1 %all-to-all-start.1 = ((bf16[8,4,128,1024]{3,2,1,0:T(8,128)(2,1)}), bf16[8,4,128,1024]{3,2,1,0:T(8,128)(2,1)}, u32[]{:S(2)}, u32[]{:S(2)}) async-start(bf16[8,4,128,1024]{3,2,1,0:T(8,128)(2,1)} %broadcast_select_fusion), calls=%async_computation.1 | async-start | bytes 16777216 | tf_op jit(solution)/shard_map/all_to_all | solution.py:400
  33.4 0.1 broadcast_bitcast_fusion
  33.5 94.3 %all-to-all-done.1 = bf16[8,4,128,1024]{3,2,1,0:T(8,128)(2,1)} async-done(((bf16[8,4,128,1024]{3,2,1,0:T(8,128)(2,1)}), bf16[8,4,128,1024]{3,2,1,0:T(8,128)(2,1)}, u32[]{:S(2)}, u32[]{:S(2)}) %all-to-all-start.1) | async-done | bytes 8388640 | tf_op jit(solution)/shard_map/all_to_all | solution.py:400
  127.8 6.2 %gather_fusion.1 = bf16[16,128,1024]{2,1,0:T(8,128)(2,1)} fusion(bf16[32,128,1024]{2,1,0:T(8,128)(2,1)} %bitcast.7, s32[1024]{0:T(1024)S(1)} %pad_clamp_fusion), kind=kCustom, calls=%fused_computation.1 | custom fusion | bytes 8388672 | tf_op jit(solution)/shard_map/jit(_take)/gather | solution.py:402
  134.0 3.8 %bitcast_select_fusion.t_ref = bf16[2048,1024]{1,0:T(8,128)(2,1)} fusion(bf16[16,128,1024]{2,1,0:T(8,128)(2,1)} %gather_fusion.1, pred[2048]{0:T(1024)(128)(4,1)S(1)} %broadcast_bitcast_fusion), kind=kLoop, calls=%fused_computation.3 | loop fusion | flops 2097152 | bytes 8390656 | tf_op jit(solution)/shard_map/jit(_take)/select_n | solution.py:402
  137.7 109.3 %train_step.1 = (bf16[512,1024]{1,0:T(8,128)(2,1)}, bf16[512,1024]{1,0:T(8,128)(2,1)}, f32[32,1024]{1,0:T(8,128)}, f32[1,1024]{1,0:T(1,128)}) custom-call(bf16[512,1024]{1,0:T(8,128)(2,1)} %x_ref.1, bf16[512,1024]{1,0:T(8,128)(2,1)} %g_ref.1, f32[1,1024]{1,0:T(1,128)} %gain_ref.1, bf16[4,1024,1024]{2,1,0:T(8,128)(2,1)} %bitcast.34, ...), custom_call_target="tpu_custom_call" | custom-call | tf_op jit(solution)/shard_map/train_step/pallas_call | solution.py:360
  247.0 0.0 copy-start
  247.0 1.2 dynamic-slice_bitcast_fusion
  248.2 2.3 copy.28
  250.5 2.3 copy.29
  252.7 0.0 copy-done
  252.7 0.7 copy.30
  (9 shorter events, 0.1 us)
Async XLA Ops:
  28.2 99.6 %all-to-all-start.1 = ((bf16[8,4,128,1024]{3,2,1,0:T(8,128)(2,1)}), bf16[8,4,128,1024]{3,2,1,0:T(8,128)(2,1)}, u32[]{:S(2)}, u32[]{:S(2)}) async-start(bf16[8,4,128,1024]{3,2,1,0:T(8,128)(2,1)} %broadcast_select_fusion), calls=%async_computation.1 | async-start | bytes 16777216 | tf_op jit(solution)/shard_map/all_to_all | solution.py:400
  247.0 5.7 %copy-start = (f32[32,1024]{1,0:T(8,128)S(1)}, f32[32,1024]{1,0:T(8,128)}, u32[]{:S(2)}) copy-start(f32[32,1024]{1,0:T(8,128)} %get-tuple-element.20) | copy-start | bytes 393220

commit v2 on v1

--- a/solution.py
+++ b/solution.py
@@ -7,10 +7,8 @@
 from jax.experimental.pallas import tpu as pltpu
 from jax.sharding import PartitionSpec as P
 
-HEADS = 16
 HD = 64
 BLOCK = 64
-BLOCKS_SEQ = 4
 CAP = 4
 SEQ = 256
 D = 1024
@@ -65,7 +63,7 @@
 
 def part_scratch(part):
     _, width, order = part
-    shapes = [pltpu.VMEM((2, 4, 4, 4, 32, width), BF16), pltpu.VMEM((4, 4, 4, 32, width), BF16)]
+    shapes = [pltpu.VMEM((4, 4, 4, 32, width), BF16)]
     dims = list(DIMS)
     n_copies = 1
     for pos, axis in enumerate(order):
@@ -78,12 +76,13 @@
     return shapes
 
 
-def reduce_part(me, part, bufs, w_out, sent):
+def reduce_part(me, part, own, bufs, w_out, sent):
     c0, width, order = part
     bufs = list(bufs)
     send_sem, recv_sem = bufs[-2:]
-    own, paired = bufs[:2]
-    pos = 2
+    paired = bufs[0]
+    pos = 1
+    cols = slice(c0, c0 + width)
     n = [0]
 
     def copy(src, dst, device):
@@ -102,7 +101,7 @@
         return cp
 
     other = along(me, "c", 1)
-    cp = copy(own.at[other], paired, moved(me, "c", 1))
+    cp = copy(own.at[other, :, :, :, :, cols], paired, moved(me, "c", 1))
     yield
     cp.wait_recv()
 
@@ -110,7 +109,7 @@
     def _(i):
         yi = lax.div(i, 4)
         zi = lax.rem(i, 4)
-        total = own[me["c"], yi, zi].astype(F32) + paired[yi, zi].astype(F32)
+        total = own[me["c"], yi, zi, :, :, cols].astype(F32) + paired[yi, zi].astype(F32)
         paired[yi, zi] = total.astype(BF16)
 
     data = paired
@@ -201,13 +200,14 @@
     return jnp.where(row >= BLOCK - 1, moved_rows, 0.0)
 
 
-def attention_block(b, q_ref, dm_ref, k_ref, v_ref, mixed_ref, dsh_ref):
+def attention_block(b, q_ref, dm_ref, kv_ref, mixed_ref, dsh_ref):
     hr = lax.broadcasted_iota(jnp.int32, (256, 256), 0) // HD
     hc = lax.broadcasted_iota(jnp.int32, (256, 256), 1) // HD
     same = hr == hc
     hcol = lax.broadcasted_iota(jnp.int32, (64, 256), 1) // HD
     qrows = pl.ds(pl.multiple_of(b * 64, 64), 64)
-    krows = pl.ds(pl.multiple_of(b * 256, 256), 256)
+    i = lax.div(b, 2)
+    n = pl.ds(lax.rem(b, 2) * 2, 2)
 
     def spread(rows):
         return jnp.where(same, jnp.concatenate([rows] * 4, axis=0), jnp.zeros((), BF16))
@@ -222,34 +222,88 @@
         cols = slice(g * 256, g * 256 + 256)
         qbd = spread(q_ref[qrows, cols])
         dobd = spread(dm_ref[qrows, cols])
-        keys = k_ref[krows, cols]
-        vals = v_ref[krows, cols]
+        keys = kv_ref[0, i, n, :, :, cols].reshape(256, 256)
+        vals = kv_ref[1, i, n, :, :, cols].reshape(256, 256)
         s = dot(keys, qbd, ((1,), (1,))) * HD ** (-0.5)
         e = jnp.exp(s - jnp.max(s, axis=0, keepdims=True))
         p = e * (1.0 / jnp.sum(e, axis=0, keepdims=True))
         pb = p.astype(BF16)
-        mixed_ref[qrows, cols] = diag(dot(pb, vals, ((0,), (0,))))
+        mixed_ref[qrows, cols] = diag(dot(pb, vals, ((0,), (0,)))).astype(BF16)
         dp = dot(vals, dobd, ((1,), (1,)))
-        v_ref[krows, cols] = dot(pb, dobd).astype(BF16)
+        kv_ref[1, i, n, :, :, cols] = dot(pb, dobd).astype(BF16).reshape(2, 4, 32, 256)
         pdp = p * dp
         rd = jnp.sum(pdp, axis=0, keepdims=True)
         ds = ((pdp - p * rd) * HD ** (-0.5)).astype(BF16)
-        dsh_ref[qrows, cols] = diag(dot(ds, keys, ((0,), (0,))))
-        k_ref[krows, cols] = dot(ds, qbd).astype(BF16)
+        dsh_ref[qrows, cols] = diag(dot(ds, keys, ((0,), (0,)))).astype(BF16)
+        kv_ref[0, i, n, :, :, cols] = dot(ds, qbd).astype(BF16).reshape(2, 4, 32, 256)
+
+
+LIB_PEERS = ((2, 0), (2, 1), (1, 0), (3, 0), (1, 1), (3, 1), (0, 1))
+
+
+def lib_peer(me, dx, dc):
+    return {**me, "x": along(me, "x", dx), "c": along(me, "c", dc)}
+
+
+def start_fetch(me, req_ref, lib_ref, asked, asked_s, stage, slots, table_sems, tile_sems):
+    mine = me["x"] * 2 + me["c"]
+    tables = []
+    for n, (dx, dc) in enumerate(LIB_PEERS):
+        cp = pltpu.make_async_remote_copy(
+            src_ref=req_ref,
+            dst_ref=asked.at[mine],
+            send_sem=table_sems.at[0, n],
+            recv_sem=table_sems.at[1, n],
+            device_id=device_of(lib_peer(me, dx, dc)),
+            device_id_type=MESH,
+        )
+        cp.start()
+        tables.append(cp)
+    asked[mine] = req_ref[...]
+    for cp in tables:
+        cp.wait_recv()
+    local = pltpu.make_async_copy(asked, asked_s, table_sems.at[0, 7])
+    local.start()
+    local.wait()
+    tiles = []
+    for n, (dx, dc) in enumerate(LIB_PEERS):
+        at = lib_peer(me, dx, dc)
+        peer = at["x"] * 2 + at["c"]
+        box = stage.at[n // 4, n % 4]
+        for k in range(CAP):
+            box[k] = lib_ref[asked_s[peer, mine, k]]
+        cp = pltpu.make_async_remote_copy(
+            src_ref=box,
+            dst_ref=slots.at[lax.div(mine, 4), lax.rem(mine, 4)],
+            send_sem=tile_sems.at[0, n],
+            recv_sem=tile_sems.at[1, n],
+            device_id=device_of(at),
+            device_id_type=MESH,
+        )
+        cp.start()
+        tiles.append(cp)
+    for k in range(CAP):
+        slots[lax.div(mine, 4), lax.rem(mine, 4), k] = lib_ref[asked_s[mine, mine, k]]
+    return tables, tiles
 
 
 def step_kernel(
-    x_ref, g_ref, gain_ref, w_ref, t_ref,
+    x_ref, g_ref, gain_ref, w_ref, lib_ref, req_ref, order_ref,
     out_ref, grad_ref, wsum_ref, gsum_ref,
-    inv_ref, normed_ref, q_ref, dm_ref, k_ref, v_ref, mixed_ref, dsh_ref, dq_ref, attn_ref,
-    tt_ref, at_ref, gslots, gsend, grecv, *part_bufs,
+    inv_ref, q_ref, dm_ref, mixed_ref, dsh_ref, dq_ref, t_ref, tt_ref, at_ref, stage, slots,
+    asked, asked_s, table_sems, tile_sems, gslots, gsend, grecv, *part_bufs,
 ):
     me = my_coords()
     barrier = pltpu.get_barrier_semaphore()
-    peers = [("c", 1)] + [(a, s) for a in ("x", "y", "z") for s in (1, 2, 3)]
-    for axis, step in peers:
-        pl.semaphore_signal(barrier, inc=1, device_id=moved(me, axis, step), device_id_type=MESH)
+    peers = [lib_peer(me, dx, dc) for dx, dc in LIB_PEERS]
+    peers += [{**me, a: along(me, a, s)} for a in ("y", "z") for s in (1, 2, 3)]
+    for at in peers:
+        pl.semaphore_signal(barrier, inc=1, device_id=device_of(at), device_id_type=MESH)
     pl.semaphore_wait(barrier, len(peers))
+
+    tables, tiles = start_fetch(
+        me, req_ref, lib_ref, asked, asked_s, stage, slots, table_sems, tile_sems
+    )
 
     @pl.loop(0, 2)
     def _(s):
@@ -258,24 +312,28 @@
         inv = lax.rsqrt(jnp.mean(x * x, axis=1, keepdims=True) + EPSILON)
         inv_ref[rows] = inv
         normed = (x * inv * gain_ref[...]).astype(BF16)
-        normed_ref[rows] = normed
+        at_ref[0, :, rows] = normed.T
         q_ref[rows] = shift_up_rows(dot(normed, w_ref[0])).astype(BF16)
         dm_ref[rows] = shift_up_rows(dot(g_ref[rows], w_ref[3], ((1,), (1,)))).astype(BF16)
 
+    for cp in tiles:
+        cp.wait_recv()
+
+    @pl.loop(0, 16)
+    def _(i):
+        o = order_ref[i]
+        t_ref[i] = slots[lax.div(o, 16), lax.rem(lax.div(o, 4), 4), lax.rem(o, 4)]
+
     @pl.loop(0, 4)
     def _(i):
-        rows = pl.ds(pl.multiple_of(i * 512, 512), 512)
-        k_ref[rows] = dot(t_ref[rows], w_ref[1]).astype(BF16)
-        v_ref[rows] = dot(t_ref[rows], w_ref[2]).astype(BF16)
+        t = t_ref[pl.ds(i * 4, 4)].reshape(512, D)
+        slots[0, i] = dot(t, w_ref[1]).astype(BF16).reshape(4, 4, 32, D)
+        slots[1, i] = dot(t, w_ref[2]).astype(BF16).reshape(4, 4, 32, D)
+        tt_ref[:, pl.ds(pl.multiple_of(i * 512, 512), 512)] = t.T
 
     @pl.loop(0, 8)
     def _(b):
-        attention_block(b, q_ref, dm_ref, k_ref, v_ref, mixed_ref, dsh_ref)
-
-    @pl.loop(0, 8)
-    def _(i):
-        rows = pl.ds(pl.multiple_of(i * 256, 256), 256)
-        tt_ref[:, rows] = t_ref[rows].T
+        attention_block(b, q_ref, dm_ref, slots, mixed_ref, dsh_ref)
 
     gslots[0] = jnp.zeros_like(gslots[0])
 
@@ -284,10 +342,10 @@
         rows = pl.ds(pl.multiple_of(s * SEQ, SEQ), SEQ)
         x = x_ref[rows].astype(F32)
         inv = inv_ref[rows]
-        attn = shift_down_rows(mixed_ref[rows]).astype(BF16)
-        attn_ref[rows] = attn
+        attn = shift_down_rows(mixed_ref[rows].astype(F32)).astype(BF16)
+        at_ref[1, :, rows] = attn.T
         out_ref[rows] = (x + dot(attn, w_ref[3])).astype(BF16)
-        dq = shift_down_rows(dsh_ref[rows]).astype(BF16)
+        dq = shift_down_rows(dsh_ref[rows].astype(F32)).astype(BF16)
         dq_ref[rows] = dq
         dn = dot(dq, w_ref[0], ((1,), (1,)))
         dnx = dn * x * inv
@@ -296,9 +354,11 @@
         inner = jnp.mean(dh * x, axis=1, keepdims=True)
         dx = inv * dh - x * (inv * inv * inv) * inner
         grad_ref[rows] = (g_ref[rows].astype(F32) + dx).astype(BF16)
-        at_ref[0, :, rows] = normed_ref[rows].T
-        at_ref[1, :, rows] = attn.T
-
+
+    for cp in tiles:
+        cp.wait_send()
+    for cp in tables:
+        cp.wait_send()
     sent = []
     n_each = len(part_bufs) // 3
     flows = [reduce_gain(me, gslots, gsend, grecv, sent)]
@@ -306,7 +366,6 @@
     for p, part in enumerate(PARTS):
         c0, width, _ = part
         bufs = part_bufs[p * n_each : (p + 1) * n_each]
-        own = bufs[0]
         cols = slice(c0, c0 + width)
 
         @pl.loop(0, 4)
@@ -315,19 +374,17 @@
             for j in range(4):
                 if j == 0:
                     res = dot(at_ref[0, rows, :], dq_ref[:, cols])
-                elif j == 1:
-                    res = dot(tt_ref[rows, :], k_ref[:, cols])
-                elif j == 2:
-                    res = dot(tt_ref[rows, :], v_ref[:, cols])
+                elif j == 3:
+                    res = dot(at_ref[1, rows, :], g_ref[:, cols])
                 else:
-                    res = dot(at_ref[1, rows, :], g_ref[:, cols])
+                    res = dot(tt_ref[rows, :], slots[j - 1, :, :, :, :, cols].reshape(2048, width))
                 res = res.astype(BF16)
                 for xi in range(4):
                     for ci in range(2):
                         r0 = (xi * 2 + ci) * 32
-                        own[ci, j, z, xi] = res[r0 : r0 + 32]
-
-        flows.append(reduce_part(me, part, bufs, wsum_ref, sent))
+                        stage[ci, j, z, xi, :, cols] = res[r0 : r0 + 32]
+
+        flows.append(reduce_part(me, part, stage, bufs, wsum_ref, sent))
         flows = [f for f in flows if next(f, True) is None]
     while flows:
         flows = [f for f in flows if next(f, True) is None]
@@ -336,20 +393,24 @@
     gsum_ref[...] = gslots[0]
 
 
-def train_step(hidden, cot, gains, weights, tiles):
+def train_step(hidden, cot, gains, weights, library, requested, order):
+    rows5 = (2, 4, 4, 4, 32, D)
     scratch = [
         pltpu.VMEM((512, 1), F32),
         pltpu.VMEM((512, D), BF16),
         pltpu.VMEM((512, D), BF16),
         pltpu.VMEM((512, D), BF16),
-        pltpu.VMEM((2048, D), BF16),
-        pltpu.VMEM((2048, D), BF16),
-        pltpu.VMEM((512, D), F32),
-        pltpu.VMEM((512, D), F32),
         pltpu.VMEM((512, D), BF16),
         pltpu.VMEM((512, D), BF16),
+        pltpu.VMEM((16, 4, 32, D), BF16),
         pltpu.VMEM((D, 2048), BF16),
         pltpu.VMEM((2, D, 512), BF16),
+        pltpu.VMEM(rows5, BF16),
+        pltpu.VMEM(rows5, BF16),
+        pltpu.VMEM((8, 8, 128), jnp.int32),
+        pltpu.SMEM((8, 8, 128), jnp.int32),
+        pltpu.SemaphoreType.DMA((2, 8)),
+        pltpu.SemaphoreType.DMA((2, 8)),
         pltpu.VMEM((15, 1, D), F32),
         pltpu.SemaphoreType.DMA((10,)),
         pltpu.SemaphoreType.DMA((10,)),
@@ -365,47 +426,37 @@
             jax.ShapeDtypeStruct((32, D), F32),
             jax.ShapeDtypeStruct((1, D), F32),
         ),
-        in_specs=[vmem] * 5,
+        in_specs=[vmem] * 6 + [pl.BlockSpec(memory_space=pltpu.SMEM)],
         out_specs=(vmem,) * 4,
         scratch_shapes=scratch,
         compiler_params=pltpu.CompilerParams(
-            collective_id=1, has_side_effects=True, vmem_limit_bytes=62 * 1024 * 1024
+            collective_id=1, has_side_effects=True, vmem_limit_bytes=63 * 1024 * 1024
         ),
         name="train_step",
-    )(hidden, cot, gains, weights, tiles)
-
-
-def fetch_tiles(library, neighbours, tile_home):
-    n_lib = lax.axis_size("lib")
-    lib_dev = library.shape[0]
+    )(hidden, cot, gains, weights, library.reshape(16, 4, 32, D), requested, order)
+
+
+def requests(neighbours, tile_home):
     home_table = tile_home[0]
     wanted = neighbours.reshape(-1)
-    n_requests = wanted.shape[0]
-    is_wanted = wanted[:, None] == jnp.arange(home_table.shape[0], dtype=jnp.int32)[None, :]
+    is_wanted = wanted[:, None] == jnp.arange(128, dtype=jnp.int32)[None, :]
     stored = jnp.sum(jnp.where(is_wanted, home_table[None, :], 0), axis=1)
-    owner_dev = stored // lib_dev
-    slot_idx = stored % lib_dev
-    req_order = jnp.arange(n_requests, dtype=jnp.int32)
-    same_before = (owner_dev[:, None] == owner_dev[None, :]) & (
-        req_order[None, :] < req_order[:, None]
+    owner = stored // 16
+    slot = stored % 16
+    i = jnp.arange(16, dtype=jnp.int32)
+    same_before = (owner[:, None] == owner[None, :]) & (i[None, :] < i[:, None])
+    rank = jnp.sum(same_before.astype(jnp.int32), axis=1)
+    hit = (owner[:, None, None] == jnp.arange(8, dtype=jnp.int32)[None, :, None]) & (
+        rank[:, None, None] == jnp.arange(128, dtype=jnp.int32)[None, None, :]
     )
-    owner_rank = jnp.sum(same_before.astype(jnp.int32), axis=1)
-    slot_hit = (owner_dev[:, None, None] == jnp.arange(n_lib, dtype=jnp.int32)[None, :, None]) & (
-        owner_rank[:, None, None] == jnp.arange(CAP, dtype=jnp.int32)[None, None, :]
+    return jnp.sum(jnp.where(hit, slot[:, None, None], 0), axis=0), owner * CAP + rank
+
+
+def body(hidden_in, cotangent, gains, weights, library, neighbours, tile_home):
+    requested, order = requests(neighbours, tile_home)
+    out, grad, w_share, g_sum = train_step(
+        hidden_in, cotangent, gains, weights[0], library, requested, order
     )
-    requested = jnp.sum(jnp.where(slot_hit, slot_idx[:, None, None], 0), axis=0)
-    asked_slots = lax.all_to_all(requested, "lib", split_axis=0, concat_axis=0, tiled=True)
-    picked = jnp.take(library, asked_slots.reshape(-1), axis=0)
-    picked = picked.reshape(asked_slots.shape + library.shape[1:])
-    arrived = lax.all_to_all(picked, "lib", split_axis=0, concat_axis=0, tiled=True)
-    slot_rows = arrived.reshape((-1,) + library.shape[1:])
-    my_tiles = jnp.take(slot_rows, owner_dev * CAP + owner_rank, axis=0)
-    return my_tiles.reshape(-1, library.shape[-1])
-
-
-def body(hidden_in, cotangent, gains, weights, library, neighbours, tile_home):
-    tiles = fetch_tiles(library, neighbours, tile_home)
-    out, grad, w_share, g_sum = train_step(hidden_in, cotangent, gains, weights[0], tiles)
     index = lax.axis_index("dp") * 8 + lax.axis_index("lib")
     g_share = lax.dynamic_slice(g_sum.reshape(-1), (index * 8,), (8,))
     return (out, grad, w_share, g_share)

time: 254 us -> 219 us (0.86)
  Pallas kernels: 109 us -> 208 us
  waiting for transfers between devices: 94.3 us -> 0 us
  local copies, waits for them, and re-layouts: 21.4 us -> 8.18 us
  other arithmetic: 13.2 us -> 2.4 us
  blocking collectives: 9.44 us -> 0 us
  starting transfers between devices: 5.14 us -> 0 us
    pallas_call x1, Pallas kernels: 109 us -> 208 us  [train_step(): pl.pallas_call(step_kernel, out_shape=(jax.ShapeDtypeStruct((512, D), BF1...]
    all_to_all x1 -> x0, waiting for transfers between devices: 94.3 us -> none  [fetch_tiles(): lax.all_to_all(picked, 'lib', split_axis=0, concat_axis=0, tiled=True)]
    gather x2 -> x0, local copies, waits for them, and re-layouts: 13.2 us -> none  [the longest x1 7.07 us: fetch_tiles(): picked = jnp.take(library, asked_slots.reshape(-1), axis=0)]
    select_n x5 -> x1, other arithmetic: 11.3 us -> 0.01 us  [requests(): owner = stored // 16]
    all_to_all x1 -> x0, blocking collectives: 9.44 us -> none  [fetch_tiles(): lax.all_to_all(requested, 'lib', split_axis=0, concat_axis=0, tiled=True)]
    all_to_all x1 -> x0, starting transfers between devices: 5.14 us -> none  [fetch_tiles(): lax.all_to_all(picked, 'lib', split_axis=0, concat_axis=0, tiled=True)]
    unnamed x6 -> x4, local copies, waits for them, and re-layouts: 5.94 us -> 6.84 us
  transfers between devices with their start and end apart: 1 -> 0, of which waited for: 1 -> 0; matrix products, arithmetic and copies ran while one was open for 0% -> 0% of each run, Pallas kernels for 0% -> 0%
where the time goes in v2:
time: 219 us
  Pallas kernels  208 us (95%)
  local copies, waits for them, and re-layouts  8.18 us (4%)
  other arithmetic  2.4 us (1%)
    pallas_call x1, Pallas kernels, train_step(): pl.pallas_call(step_kernel, out_shape=(jax.ShapeDtypeStruct((512, D), BF1...  208 us
    unnamed x4, local copies, waits for them, and re-layouts  6.84 us

profile of v2, /device:TPU:0, one launch (start us, length us, event | category | flops | bytes accessed | tf_op | source)
XLA Modules:
  0.0 219.0 jit_solution(6980322777767506652)
XLA Ops:
  0.6 0.8 copy.13
  1.4 0.1 eq.66
  1.5 0.8 select_reduce_fusion.1
  2.3 0.2 convert_reduce_fusion
  2.5 0.5 multiply_add_fusion.order_ref
  3.0 0.1 iota_compare_fusion.2
  3.1 0.1 iota_compare_fusion
  3.2 0.7 select_reduce_fusion.req_ref
  3.9 207.7 %train_step.1 = (bf16[512,1024]{1,0:T(8,128)(2,1)}, bf16[512,1024]{1,0:T(8,128)(2,1)}, f32[32,1024]{1,0:T(8,128)}, f32[1,1024]{1,0:T(1,128)}) custom-call(bf16[512,1024]{1,0:T(8,128)(2,1)} %x_ref.1, bf16[512,1024]{1,0:T(8,128)(2,1)} %g_ref.1, f32[1,1024]{1,0:T(1,128)} %gain_ref.1, bf16[4,1024,1024]{2,1,0:T(8,128)(2,1)} %bitcast.5, ...), custom_call_target="tpu_custom_call" | custom-call | tf_op jit(solution)/shard_map/train_step/pallas_call | solution.py:421
  211.6 1.3 dynamic-slice_bitcast_fusion
  212.9 2.3 %copy.17 = bf16[512,1024]{1,0:T(8,128)(2,1)} copy(bf16[512,1024]{1,0:T(8,128)(2,1)} %get-tuple-element.18) | data formatting | bytes 2097152
  215.1 2.3 %copy.18 = bf16[512,1024]{1,0:T(8,128)(2,1)} copy(bf16[512,1024]{1,0:T(8,128)(2,1)} %get-tuple-element.19) | data formatting | bytes 2097152
  217.4 1.6 copy.19
  (1 shorter events, 0.0 us)

commit v3 on v2

v3 whole, which is shorter than its diff:
```python
import functools

import jax
import jax.numpy as jnp
from jax import lax
from jax.experimental import pallas as pl
from jax.experimental.pallas import tpu as pltpu
from jax.sharding import PartitionSpec as P

HD = 64
BLOCK = 64
CAP = 4
SEQ = 256
D = 1024
EPSILON = 1e-06

F32 = jnp.float32
BF16 = jnp.bfloat16
MESH = pl.DeviceIdType.MESH

ORDERS = (
    ("x", "y", "z"),
    ("y", "z", "x"),
    ("z", "x", "y"),
    ("x", "z", "y"),
    ("y", "x", "z"),
    ("z", "y", "x"),
    ("x", "y", "z"),
    ("z", "x", "y"),
)
PARTS = 4
DIMS = ("y", "z", "x")


def dot(left, right, dims=((1,), (0,))):
    return lax.dot_general(left, right, (dims, ((), ())), preferred_element_type=F32)


def my_coords():
    dp = lax.axis_index("dp")
    lib = lax.axis_index("lib")
    return {
        "y": lax.div(dp, 4),
        "z": lax.rem(dp, 4),
        "x": lax.div(lib, 2),
        "c": lax.rem(lib, 2),
    }


def device_of(at):
    return (at["y"] * 4 + at["z"], at["x"] * 2 + at["c"])


def along(me, axis, step):
    size = 2 if axis == "c" else 4
    return lax.rem(me[axis] + step, size)


def moved(me, axis, step):
    return device_of({**me, axis: along(me, axis, step)})


def piece_scratch():
    shapes = []
    for left in (2, 1, 0):
        block = (4,) * left + (32, 128)
        shapes.append(pltpu.VMEM((3,) + block, BF16))
        if left:
            shapes.append(pltpu.VMEM(block, BF16))
    shapes.append(pltpu.SemaphoreType.DMA((2, 9)))
    return shapes


def part_scratch():
    return [pltpu.VMEM((4, 4, 4, 32, 256), BF16), pltpu.SemaphoreType.DMA((2,))]


def start_pair(me, p, own, paired, sems):
    cols = slice(p * 256, p * 256 + 256)
    cp = pltpu.make_async_remote_copy(
        src_ref=own.at[along(me, "c", 1), :, :, :, :, cols],
        dst_ref=paired,
        send_sem=sems.at[0],
        recv_sem=sems.at[1],
        device_id=moved(me, "c", 1),
        device_id_type=MESH,
    )
    cp.start()
    return cp


def end_pair(me, p, own, paired, cp):
    cols = slice(p * 256, p * 256 + 256)
    cp.wait_recv()

    @pl.loop(0, 16)
    def _(i):
        yi = lax.div(i, 4)
        zi = lax.rem(i, 4)
        total = own[me["c"], yi, zi, :, :, cols].astype(F32) + paired[yi, zi].astype(F32)
        paired[yi, zi] = total.astype(BF16)


def reduce_piece(me, q, data, bufs, w_out, sent):
    sems = bufs[-1]
    dims = list(DIMS)
    n = 0
    for pos, axis in enumerate(ORDERS[q]):
        recv = bufs[2 * pos]
        at = dims.index(axis)

        def chunk(step):
            idx = [slice(None)] * len(dims)
            idx[at] = along(me, axis, step)
            return tuple(idx)

        cps = []
        for step in (2, 1, 3):
            cp = pltpu.make_async_remote_copy(
                src_ref=data.at[chunk(step)],
                dst_ref=recv.at[step - 1],
                send_sem=sems.at[0, n],
                recv_sem=sems.at[1, n],
                device_id=moved(me, axis, step),
                device_id_type=MESH,
            )
            cp.start()
            sent.append(cp)
            cps.append(cp)
            n += 1
        yield
        for cp in cps:
            cp.wait_recv()
        total = data[chunk(0)].astype(F32)
        for k in range(3):
            total = total + recv[k].astype(F32)
        if pos < 2:
            data = bufs[2 * pos + 1]
            data[...] = total.astype(BF16)
        else:
            w_out[:, q * 128 : q * 128 + 128] = total
        dims.remove(axis)


def reduce_gain(me, slots, send_sem, recv_sem, sent):
    k = 0
    for stage, axis in enumerate(("lib", "y", "z"), 1):
        if axis == "lib":
            peers = [lib_peer(me, dx, dc) for dx, dc in LIB_PEERS]
        else:
            peers = [{**me, axis: along(me, axis, step)} for step in (1, 2, 3)]
        slots[stage] = slots[0]
        cps = []
        first = k
        for at in peers:
            cp = pltpu.make_async_remote_copy(
                src_ref=slots.at[stage],
                dst_ref=slots.at[4 + k],
                send_sem=send_sem.at[k],
                recv_sem=recv_sem.at[k],
                device_id=device_of(at),
                device_id_type=MESH,
            )
            cp.start()
            sent.append(cp)
            cps.append(cp)
            k += 1
        yield
        total = slots[stage]
        for i, cp in enumerate(cps):
            cp.wait_recv()
            total = total + slots[4 + first + i]
        slots[0] = total


def shift_up_rows(rows):
    moved_rows = pltpu.roll(rows, SEQ - (BLOCK - 1), 0)
    row = lax.broadcasted_iota(jnp.int32, rows.shape, 0)
    return jnp.where(row < SEQ - BLOCK + 1, moved_rows, 0.0)


def shift_down_rows(rows):
    moved_rows = pltpu.roll(rows, BLOCK - 1, 0)
    row = lax.broadcasted_iota(jnp.int32, rows.shape, 0)
    return jnp.where(row >= BLOCK - 1, moved_rows, 0.0)


def attention_block(b, q_ref, dm_ref, kv_ref, mixed_ref, dsh_ref):
    hr = lax.broadcasted_iota(jnp.int32, (256, 256), 0) // HD
    hc = lax.broadcasted_iota(jnp.int32, (256, 256), 1) // HD
    same = hr == hc
    hcol = lax.broadcasted_iota(jnp.int32, (64, 256), 1) // HD
    qrows = pl.ds(pl.multiple_of(b * 64, 64), 64)
    i = lax.div(b, 2)
    n = pl.ds(lax.rem(b, 2) * 2, 2)

    def spread(rows):
        return jnp.where(same, jnp.concatenate([rows] * 4, axis=0), jnp.zeros((), BF16))

    def diag(full):
        out = full[0:64]
        for h in range(1, 4):
            out = jnp.where(hcol == h, full[h * 64 : h * 64 + 64], out)
        return out

    groups = [slice(g * 256, g * 256 + 256) for g in range(4)]
    qbd = [spread(q_ref[qrows, c]) for c in groups]
    dobd = [spread(dm_ref[qrows, c]) for c in groups]
    keys = [kv_ref[0, i, n, :, :, c].reshape(256, 256) for c in groups]
    vals = [kv_ref[1, i, n, :, :, c].reshape(256, 256) for c in groups]
    score = [dot(k, q, ((1,), (1,))) * HD ** (-0.5) for k, q in zip(keys, qbd)]
    dp = [dot(v, d, ((1,), (1,))) for v, d in zip(vals, dobd)]
    e = [jnp.exp(a - jnp.max(a, axis=0, keepdims=True)) for a in score]
    p = [a * (1.0 / jnp.sum(a, axis=0, keepdims=True)) for a in e]
    pb = [a.astype(BF16) for a in p]
    pdp = [a * d for a, d in zip(p, dp)]
    rd = [jnp.sum(a, axis=0, keepdims=True) for a in pdp]
    ds = [((a - w * r) * HD ** (-0.5)).astype(BF16) for a, w, r in zip(pdp, p, rd)]
    mixed = [diag(dot(a, v, ((0,), (0,)))).astype(BF16) for a, v in zip(pb, vals)]
    dv = [dot(a, d).astype(BF16).reshape(2, 4, 32, 256) for a, d in zip(pb, dobd)]
    dsh = [diag(dot(a, k, ((0,), (0,)))).astype(BF16) for a, k in zip(ds, keys)]
    dk = [dot(a, q).astype(BF16).reshape(2, 4, 32, 256) for a, q in zip(ds, qbd)]
    for g, c in enumerate(groups):
        mixed_ref[qrows, c] = mixed[g]
        dsh_ref[qrows, c] = dsh[g]
        kv_ref[1, i, n, :, :, c] = dv[g]
        kv_ref[0, i, n, :, :, c] = dk[g]


LIB_PEERS = ((2, 0), (2, 1), (1, 0), (3, 0), (1, 1), (3, 1), (0, 1))


def lib_peer(me, dx, dc):
    return {**me, "x": along(me, "x", dx), "c": along(me, "c", dc)}


def start_fetch(me, req_ref, lib_ref, lib_load, asked, asked_s, stage, slots, table_sems, tile_sems):
    mine = me["x"] * 2 + me["c"]
    tables = []
    for n, (dx, dc) in enumerate(LIB_PEERS):
        cp = pltpu.make_async_remote_copy(
            src_ref=req_ref,
            dst_ref=asked.at[mine],
            send_sem=table_sems.at[0, n],
            recv_sem=table_sems.at[1, n],
            device_id=device_of(lib_peer(me, dx, dc)),
            device_id_type=MESH,
        )
        cp.start()
        tables.append(cp)
    asked[mine] = req_ref[...]
    for cp in tables:
        cp.wait_recv()
    local = pltpu.make_async_copy(asked, asked_s, table_sems.at[0, 7])
    local.start()
    local.wait()
    lib_load.wait()
    tiles = []
    for n, (dx, dc) in enumerate(LIB_PEERS):
        at = lib_peer(me, dx, dc)
        peer = at["x"] * 2 + at["c"]
        box = stage.at[n // 4, n % 4]
        for k in range(CAP):
            box[k] = lib_ref[asked_s[peer, mine, k]]
        cp = pltpu.make_async_remote_copy(
            src_ref=box,
            dst_ref=slots.at[lax.div(mine, 4), lax.rem(mine, 4)],
            send_sem=tile_sems.at[0, n],
            recv_sem=tile_sems.at[1, n],
            device_id=device_of(at),
            device_id_type=MESH,
        )
        cp.start()
        tiles.append(cp)
    for k in range(CAP):
        slots[lax.div(mine, 4), lax.rem(mine, 4), k] = lib_ref[asked_s[mine, mine, k]]
    return tables, tiles


def step_kernel(
    x_hbm, g_hbm, gain_ref, w_hbm, lib_hbm, req_ref, order_ref,
    out_ref, grad_ref, wsum_ref, gsum_ref,
    x_ref, g_ref, w_ref, lib_ref, load_sems,
    inv_ref, q_ref, dm_ref, mixed_ref, dsh_ref, t_ref, tt_ref, at_ref, stage, slots,
    asked, asked_s, table_sems, tile_sems, gslots, gsend, grecv, *sum_bufs,
):
    me = my_coords()
    loads = []
    pairs = [(lib_hbm, lib_ref), (x_hbm, x_ref), (w_hbm.at[0], w_ref.at[0]), (g_hbm, g_ref)]
    pairs += [(w_hbm.at[j], w_ref.at[j]) for j in (3, 1, 2)]
    for n, (src, dst) in enumerate(pairs):
        cp = pltpu.make_async_copy(src, dst, load_sems.at[n])
        cp.start()
        loads.append(cp)

    barrier = pltpu.get_barrier_semaphore()
    peers = [lib_peer(me, dx, dc) for dx, dc in LIB_PEERS]
    peers += [{**me, a: along(me, a, s)} for a in ("y", "z") for s in (1, 2, 3)]
    for at in peers:
        pl.semaphore_signal(barrier, inc=1, device_id=device_of(at), device_id_type=MESH)
    pl.semaphore_wait(barrier, len(peers))

    tables, tiles = start_fetch(
        me, req_ref, lib_ref, loads[0], asked, asked_s, stage, slots, table_sems, tile_sems
    )

    for cp in loads[1:5]:
        cp.wait()

    @pl.loop(0, 2)
    def _(s):
        rows = pl.ds(pl.multiple_of(s * SEQ, SEQ), SEQ)
        x = x_ref[rows].astype(F32)
        inv = lax.rsqrt(jnp.mean(x * x, axis=1, keepdims=True) + EPSILON)
        inv_ref[rows] = inv
        normed = (x * inv * gain_ref[...]).astype(BF16)
        at_ref[0, :, rows] = normed.T
        q_ref[rows] = shift_up_rows(dot(normed, w_ref[0])).astype(BF16)
        dm_ref[rows] = shift_up_rows(dot(g_ref[rows], w_ref[3], ((1,), (1,)))).astype(BF16)

    for cp in loads[5:]:
        cp.wait()
    for cp in tiles:
        cp.wait_recv()

    @pl.loop(0, 16)
    def _(i):
        o = order_ref[i]
        t_ref[i] = slots[lax.div(o, 16), lax.rem(lax.div(o, 4), 4), lax.rem(o, 4)]

    @pl.loop(0, 4)
    def _(i):
        t = t_ref[pl.ds(i * 4, 4)].reshape(512, D)
        slots[0, i] = dot(t, w_ref[1]).astype(BF16).reshape(4, 4, 32, D)
        slots[1, i] = dot(t, w_ref[2]).astype(BF16).reshape(4, 4, 32, D)
        tt_ref[:, pl.ds(pl.multiple_of(i * 512, 512), 512)] = t.T

    @pl.loop(0, 8)
    def _(b):
        attention_block(b, q_ref, dm_ref, slots, mixed_ref, dsh_ref)

    @pl.loop(0, 2)
    def _(s):
        rows = pl.ds(pl.multiple_of(s * SEQ, SEQ), SEQ)
        attn = shift_down_rows(mixed_ref[rows].astype(F32)).astype(BF16)
        mixed_ref[rows] = attn
        at_ref[1, :, rows] = attn.T
        dsh_ref[rows] = shift_down_rows(dsh_ref[rows].astype(F32)).astype(BF16)

    for cp in tiles:
        cp.wait_send()
    for cp in tables:
        cp.wait_send()

    def weight_terms(p):
        cols = slice(p * 256, p * 256 + 256)

        @pl.loop(0, 4)
        def _(z):
            rows = pl.ds(pl.multiple_of(z * 256, 256), 256)
            for j in range(4):
                if j == 0:
                    res = dot(at_ref[0, rows, :], dsh_ref[:, cols])
                elif j == 3:
                    res = dot(at_ref[1, rows, :], g_ref[:, cols])
                else:
                    res = dot(tt_ref[rows, :], slots[j - 1, :, :, :, :, cols].reshape(2048, 256))
                res = res.astype(BF16)
                for xi in range(4):
                    for ci in range(2):
                        r0 = (xi * 2 + ci) * 32
                        stage[ci, j, z, xi, :, cols] = res[r0 : r0 + 32]

    def row_results(s):
        rows = pl.ds(s * SEQ, SEQ)
        x = x_ref[rows].astype(F32)
        inv = inv_ref[rows]
        out_ref[rows] = (x + dot(mixed_ref[rows], w_ref[3])).astype(BF16)
        dn = dot(dsh_ref[rows], w_ref[0], ((1,), (1,)))
        dnx = dn * x * inv
        term = jnp.sum(dnx, axis=0, keepdims=True)
        gslots[0] = term if s == 0 else gslots[0] + term
        dh = dn * gain_ref[...]
        inner = jnp.mean(dh * x, axis=1, keepdims=True)
        dx = inv * dh - x * (inv * inv * inv) * inner
        grad_ref[rows] = (g_ref[rows].astype(F32) + dx).astype(BF16)

    sent = []
    part_bufs = sum_bufs[: 2 * PARTS]
    piece_bufs = sum_bufs[2 * PARTS :]
    n_each = len(piece_bufs) // (2 * PARTS)
    pair = {}
    flow = {}

    def send_part(p):
        pair[p] = start_pair(me, p, stage, *part_bufs[2 * p : 2 * p + 2])
        sent.append(pair[p])

    def sum_part(p):
        paired = part_bufs[2 * p]
        end_pair(me, p, stage, paired, pair[p])
        flow[p] = []
        for h in range(2):
            q = 2 * p + h
            bufs = piece_bufs[q * n_each : (q + 1) * n_each]
            data = paired.at[:, :, :, :, pl.ds(h * 128, 128)]
            flow[p].append(reduce_piece(me, q, data, bufs, wsum_ref, sent))
            next(flow[p][-1])

    def advance(p):
        for f in flow[p]:
            next(f, None)

    weight_terms(0)
    send_part(0)
    weight_terms(1)
    send_part(1)
    sum_part(0)
    weight_terms(2)
    send_part(2)
    sum_part(1)
    weight_terms(3)
    send_part(3)
    sum_part(2)
    advance(0)
    row_results(0)
    sum_part(3)
    advance(1)
    advance(0)
    row_results(1)
    gain_flow = reduce_gain(me, gslots, gsend, grecv, sent)
    next(gain_flow)
    advance(2)
    advance(1)
    advance(0)
    next(gain_flow)
    advance(3)
    advance(2)
    advance(1)
    next(gain_flow)
    advance(3)
    advance(2)
    next(gain_flow, None)
    advance(3)
    for cp in sent:
        cp.wait_send()
    index = lax.axis_index("dp") * 8 + lax.axis_index("lib")
    gsum_ref[...] = pltpu.roll(gslots[0], lax.rem(D - index * 8, D), 1)[:, :128]


def train_step(hidden, cot, gains, weights, library, requested, order):
    rows5 = (2, 4, 4, 4, 32, D)
    scratch = [
        pltpu.VMEM((512, D), BF16),
        pltpu.VMEM((512, D), BF16),
        pltpu.VMEM((4, D, D), BF16),
        pltpu.VMEM((16, 4, 32, D), BF16),
        pltpu.SemaphoreType.DMA((7,)),
        pltpu.VMEM((512, 1), F32),
        pltpu.VMEM((512, D), BF16),
        pltpu.VMEM((512, D), BF16),
        pltpu.VMEM((512, D), BF16),
        pltpu.VMEM((512, D), BF16),
        pltpu.VMEM((16, 4, 32, D), BF16),
        pltpu.VMEM((D, 2048), BF16),
        pltpu.VMEM((2, D, 512), BF16),
        pltpu.VMEM(rows5, BF16),
        pltpu.VMEM(rows5, BF16),
        pltpu.VMEM((8, 8, 128), jnp.int32),
        pltpu.SMEM((8, 8, 128), jnp.int32),
        pltpu.SemaphoreType.DMA((2, 8)),
        pltpu.SemaphoreType.DMA((2, 8)),
        pltpu.VMEM((17, 1, D), F32),
        pltpu.SemaphoreType.DMA((13,)),
        pltpu.SemaphoreType.DMA((13,)),
    ]
    for _ in range(PARTS):
        scratch += part_scratch()
    for _ in range(2 * PARTS):
        scratch += piece_scratch()
    hbm = pl.BlockSpec(memory_space=pl.ANY)
    vmem = pl.BlockSpec(memory_space=pltpu.VMEM)
    return pl.pallas_call(
        step_kernel,
        out_shape=(
            jax.ShapeDtypeStruct((512, D), BF16),
            jax.ShapeDtypeStruct((512, D), BF16),
            jax.ShapeDtypeStruct((32, D), F32),
            jax.ShapeDtypeStruct((1, 128), F32),
        ),
        in_specs=[hbm, hbm, vmem, hbm, hbm, vmem, pl.BlockSpec(memory_space=pltpu.SMEM)],
        out_specs=(vmem,) * 4,
        scratch_shapes=scratch,
        compiler_params=pltpu.CompilerParams(
            collective_id=1, has_side_effects=True, vmem_limit_bytes=63 * 1024 * 1024
        ),
        name="train_step",
    )(hidden, cot, gains, weights, library.reshape(16, 4, 32, D), requested, order)


def requests(neighbours, tile_home):
    home_table = tile_home[0]
    wanted = neighbours.reshape(-1)
    is_wanted = wanted[:, None] == jnp.arange(128, dtype=jnp.int32)[None, :]
    stored = jnp.sum(jnp.where(is_wanted, home_table[None, :], 0), axis=1)
    owner = stored // 16
    slot = stored % 16
    i = jnp.arange(16, dtype=jnp.int32)
    same_before = (owner[:, None] == owner[None, :]) & (i[None, :] < i[:, None])
    rank = jnp.sum(same_before.astype(jnp.int32), axis=1)
    hit = (owner[:, None, None] == jnp.arange(8, dtype=jnp.int32)[None, :, None]) & (
        rank[:, None, None] == jnp.arange(128, dtype=jnp.int32)[None, None, :]
    )
    return jnp.sum(jnp.where(hit, slot[:, None, None], 0), axis=0), owner * CAP + rank


def body(hidden_in, cotangent, gains, weights, library, neighbours, tile_home):
    requested, order = requests(neighbours, tile_home)
    out, grad, w_share, g_sum = train_step(
        hidden_in, cotangent, gains, weights[0], library, requested, order
    )
    g_share = g_sum[0, :8]
    return (out, grad, w_share, g_share)


def solution(mesh):
    return jax.shard_map(
        body,
        mesh=mesh,
        in_specs=(
            P(("dp", "lib"), None),
            P(("dp", "lib"), None),
            P(),
            P(),
            P(("dp", "lib"), None, None),
            P(("dp", "lib"), None),
            P("dp", None),
        ),
        out_specs=(
            P(("dp", "lib"), None),
            P(("dp", "lib"), None),
            P(("dp", "lib"), None),
            P(("dp", "lib")),
        ),
        check_vma=False,
    )
```

time: 219 us -> 183 us (0.84)
  Pallas kernels: 208 us -> 172 us
    pallas_call x1, Pallas kernels: 208 us -> 172 us  [train_step(): pl.pallas_call(step_kernel, out_shape=(jax.ShapeDtypeStruct((512, D), BF1...]
where the time goes in v3:
time: 183 us
  Pallas kernels  172 us (94%)
  local copies, waits for them, and re-layouts  8.1 us (4%)
  other arithmetic  2.4 us (1%)
    pallas_call x1, Pallas kernels, train_step(): pl.pallas_call(step_kernel, out_shape=(jax.ShapeDtypeStruct((512, D), BF1...  172 us
    unnamed x4, local copies, waits for them, and re-layouts  6.84 us

profile of v3, /device:TPU:0, one launch (start us, length us, event | category | flops | bytes accessed | tf_op | source)
XLA Modules:
  0.0 182.9 jit_solution(11859407459151704416)
XLA Ops:
  0.6 0.8 copy.13
  1.4 0.1 eq.66
  1.5 0.8 select_reduce_fusion.1
  2.3 0.2 convert_reduce_fusion
  2.5 0.5 multiply_add_fusion.order_ref
  3.0 0.1 iota_compare_fusion.2
  3.1 0.1 iota_compare_fusion
  3.2 0.7 select_reduce_fusion.req_ref
  3.9 171.8 %train_step.1 = (bf16[512,1024]{1,0:T(8,128)(2,1)}, bf16[512,1024]{1,0:T(8,128)(2,1)}, f32[32,1024]{1,0:T(8,128)}, f32[1,128]{1,0:T(1,128)}) custom-call(bf16[512,1024]{1,0:T(8,128)(2,1)} %x_hbm.1, bf16[512,1024]{1,0:T(8,128)(2,1)} %g_hbm.1, f32[1,1024]{1,0:T(1,128)} %gain_ref.1, bf16[4,1024,1024]{2,1,0:T(8,128)(2,1)} %bitcast.5, ...), custom_call_target="tpu_custom_call" | custom-call | tf_op jit(solution)/shard_map/train_step/pallas_call | solution.py:483
  175.7 1.2 slice_bitcast_fusion
  176.9 2.3 %copy.17 = bf16[512,1024]{1,0:T(8,128)(2,1)} copy(bf16[512,1024]{1,0:T(8,128)(2,1)} %get-tuple-element.18) | data formatting | bytes 2097152
  179.1 2.3 %copy.18 = bf16[512,1024]{1,0:T(8,128)(2,1)} copy(bf16[512,1024]{1,0:T(8,128)(2,1)} %get-tuple-element.19) | data formatting | bytes 2097152
  181.4 1.6 copy.19
  (1 shorter events, 0.0 us)

commit v4 on v3

v4 whole, which is shorter than its diff:
```python
import functools

import jax
import jax.numpy as jnp
from jax import lax
from jax.experimental import pallas as pl
from jax.experimental.pallas import tpu as pltpu
from jax.sharding import PartitionSpec as P

HD = 64
BLOCK = 64
CAP = 4
SEQ = 256
D = 1024
EPSILON = 1e-06

F32 = jnp.float32
BF16 = jnp.bfloat16
MESH = pl.DeviceIdType.MESH

ORDERS = (
    ("x", "y", "z"),
    ("y", "z", "x"),
    ("z", "x", "y"),
    ("x", "z", "y"),
    ("y", "x", "z"),
    ("z", "y", "x"),
    ("x", "y", "z"),
    ("z", "x", "y"),
)
PARTS = 4
DIMS = ("y", "z", "x")


def dot(left, right, dims=((1,), (0,))):
    return lax.dot_general(left, right, (dims, ((), ())), preferred_element_type=F32)


def my_coords():
    dp = lax.axis_index("dp")
    lib = lax.axis_index("lib")
    return {
        "y": lax.div(dp, 4),
        "z": lax.rem(dp, 4),
        "x": lax.div(lib, 2),
        "c": lax.rem(lib, 2),
    }


def device_of(at):
    return (at["y"] * 4 + at["z"], at["x"] * 2 + at["c"])


def along(me, axis, step):
    size = 2 if axis == "c" else 4
    return lax.rem(me[axis] + step, size)


def moved(me, axis, step):
    return device_of({**me, axis: along(me, axis, step)})


def piece_scratch():
    shapes = []
    for left in (2, 1, 0):
        block = (4,) * left + (32, 128)
        shapes.append(pltpu.VMEM((3,) + block, BF16))
    shapes.append(pltpu.SemaphoreType.DMA((2, 9)))
    return shapes


def start_pair(me, p, own, paired, sems):
    cols = slice(p * 256, p * 256 + 256)
    cp = pltpu.make_async_remote_copy(
        src_ref=own.at[along(me, "c", 1), :, :, :, :, cols],
        dst_ref=paired.at[:, :, :, :, cols],
        send_sem=sems.at[0, p],
        recv_sem=sems.at[1, p],
        device_id=moved(me, "c", 1),
        device_id_type=MESH,
    )
    cp.start()
    return cp


def end_pair(me, p, own, paired, cp):
    cols = slice(p * 256, p * 256 + 256)
    cp.wait_recv()

    @pl.loop(0, 16)
    def _(i):
        yi = lax.div(i, 4)
        zi = lax.rem(i, 4)
        total = own[me["c"], yi, zi, :, :, cols].astype(F32)
        total = total + paired[yi, zi, :, :, cols].astype(F32)
        paired[yi, zi, :, :, cols] = total.astype(BF16)


def reduce_piece(me, q, data, bufs, w_out, sent):
    sems = bufs[-1]
    dims = list(DIMS)
    n = 0
    for pos, axis in enumerate(ORDERS[q]):
        recv = bufs[pos]
        at = dims.index(axis)

        def chunk(step):
            idx = [slice(None)] * len(dims)
            idx[at] = along(me, axis, step)
            return tuple(idx)

        cps = []
        for step in (2, 1, 3):
            cp = pltpu.make_async_remote_copy(
                src_ref=data.at[chunk(step)],
                dst_ref=recv.at[step - 1],
                send_sem=sems.at[0, n],
                recv_sem=sems.at[1, n],
                device_id=moved(me, axis, step),
                device_id_type=MESH,
            )
            cp.start()
            sent.append(cp)
            cps.append(cp)
            n += 1
        yield
        for cp in cps:
            cp.wait_recv()
        total = data[chunk(0)].astype(F32)
        for k in range(3):
            total = total + recv[k].astype(F32)
        if pos < 2:
            data = recv.at[0]
            data[...] = total.astype(BF16)
        else:
            w_out[:, q * 128 : q * 128 + 128] = total
        dims.remove(axis)


def reduce_gain(me, slots, send_sem, recv_sem, sent):
    k = 0
    for stage, axis in enumerate(("lib", "y", "z"), 1):
        if axis == "lib":
            peers = [lib_peer(me, dx, dc) for dx, dc in LIB_PEERS]
        else:
            peers = [{**me, axis: along(me, axis, step)} for step in (1, 2, 3)]
        slots[stage] = slots[0]
        cps = []
        first = k
        for at in peers:
            cp = pltpu.make_async_remote_copy(
                src_ref=slots.at[stage],
                dst_ref=slots.at[4 + k],
                send_sem=send_sem.at[k],
                recv_sem=recv_sem.at[k],
                device_id=device_of(at),
                device_id_type=MESH,
            )
            cp.start()
            sent.append(cp)
            cps.append(cp)
            k += 1
        yield
        total = slots[stage]
        for i, cp in enumerate(cps):
            cp.wait_recv()
            total = total + slots[4 + first + i]
        slots[0] = total


def shift_up_rows(rows):
    moved_rows = pltpu.roll(rows, SEQ - (BLOCK - 1), 0)
    row = lax.broadcasted_iota(jnp.int32, rows.shape, 0)
    return jnp.where(row < SEQ - BLOCK + 1, moved_rows, 0.0)


def shift_down_rows(rows):
    moved_rows = pltpu.roll(rows, BLOCK - 1, 0)
    row = lax.broadcasted_iota(jnp.int32, rows.shape, 0)
    return jnp.where(row >= BLOCK - 1, moved_rows, 0.0)


def head_of(shape, dim):
    return lax.broadcasted_iota(jnp.int32, shape, dim) // HD


def spread(rows):
    same = head_of((256, 256), 0) == head_of((256, 256), 1)
    return jnp.where(same, jnp.concatenate([rows] * 4, axis=0), jnp.zeros((), BF16))


def diag(full):
    hcol = head_of((64, 256), 1)
    out = full[0:64]
    for h in range(1, 4):
        out = jnp.where(hcol == h, full[h * 64 : h * 64 + 64], out)
    return out


def block_rows(b):
    return pl.ds(pl.multiple_of(b * 64, 64), 64)


def block_tiles(b):
    return lax.div(b, 2), pl.ds(lax.rem(b, 2) * 2, 2)


def slot_rows(ref, order_ref, b, c):
    tiles = [ref[order_ref[b * 2 + n], :, :, c].reshape(128, 256) for n in range(2)]
    return jnp.concatenate(tiles, axis=0)


def attend(b, order_ref, q_ref, k_ref, v_ref, prob_ref, mixed_ref):
    groups = [slice(g * 256, g * 256 + 256) for g in range(4)]
    rows = block_rows(b)
    qbd = [spread(q_ref[rows, c]) for c in groups]
    keys = [slot_rows(k_ref, order_ref, b, c) for c in groups]
    vals = [slot_rows(v_ref, order_ref, b, c) for c in groups]
    score = [dot(k, q, ((1,), (1,))) * HD ** (-0.5) for k, q in zip(keys, qbd)]
    e = [jnp.exp(a - jnp.max(a, axis=0, keepdims=True)) for a in score]
    pb = [(a * (1.0 / jnp.sum(a, axis=0, keepdims=True))).astype(BF16) for a in e]
    mixed = [diag(dot(a, v, ((0,), (0,)))).astype(BF16) for a, v in zip(pb, vals)]
    for g, c in enumerate(groups):
        prob_ref[pl.ds(b * 2, 2), :, :, c] = pb[g].reshape(2, 4, 32, 256)
        mixed_ref[rows, c] = mixed[g]


def attend_back(b0, n_blocks, g, order_ref, q_ref, dm_ref, k_ref, v_ref, prob_ref, dkv_ref, dsh_ref):
    c = slice(g * 256, g * 256 + 256)
    blocks = [b0 + k for k in range(n_blocks)]
    at = [block_tiles(b) for b in blocks]
    qbd = [spread(q_ref[block_rows(b), c]) for b in blocks]
    dobd = [spread(dm_ref[block_rows(b), c]) for b in blocks]
    keys = [slot_rows(k_ref, order_ref, b, c) for b in blocks]
    vals = [slot_rows(v_ref, order_ref, b, c) for b in blocks]
    pb = [prob_ref[pl.ds(b * 2, 2), :, :, c].reshape(256, 256) for b in blocks]
    dp = [dot(v, d, ((1,), (1,))) for v, d in zip(vals, dobd)]
    dv = [dot(a, d).astype(BF16).reshape(2, 4, 32, 256) for a, d in zip(pb, dobd)]
    p = [a.astype(F32) for a in pb]
    pdp = [a * d for a, d in zip(p, dp)]
    rd = [
        jnp.sum(w, axis=0, keepdims=True) * (1.0 / jnp.sum(a, axis=0, keepdims=True))
        for w, a in zip(pdp, p)
    ]
    ds = [((w - a * r) * HD ** (-0.5)).astype(BF16) for w, a, r in zip(pdp, p, rd)]
    dsh = [diag(dot(a, k, ((0,), (0,)))).astype(BF16) for a, k in zip(ds, keys)]
    dk = [dot(a, q).astype(BF16).reshape(2, 4, 32, 256) for a, q in zip(ds, qbd)]
    for k, b in enumerate(blocks):
        i, n = at[k]
        dsh_ref[block_rows(b), c] = dsh[k]
        dkv_ref[1, i, n, :, :, c] = dv[k]
        dkv_ref[0, i, n, :, :, c] = dk[k]


LIB_PEERS = ((2, 0), (2, 1), (1, 0), (3, 0), (1, 1), (3, 1), (0, 1))


def lib_peer(me, dx, dc):
    return {**me, "x": along(me, "x", dx), "c": along(me, "c", dc)}


def request_table(wanted, home, order):
    row = lax.broadcasted_iota(jnp.int32, (8, 128), 0)
    col = lax.broadcasted_iota(jnp.int32, (8, 128), 1)
    table = jnp.zeros((8, 128), jnp.int32)
    owners = []
    for i in range(16):
        stored = home[0, wanted[i // 2, i % 2]]
        owner = lax.div(stored, 16)
        rank = jnp.int32(0)
        for before in owners:
            rank = rank + jnp.where(before == owner, 1, 0)
        owners.append(owner)
        order[i] = owner * CAP + rank
        table = jnp.where((row == owner) & (col == rank), lax.rem(stored, 16), table)
    return table


def start_fetch(me, req_ref, lib_ref, loads, asked, asked_s, stage, slots, table_sems, tile_sems):
    mine = me["x"] * 2 + me["c"]
    tables = []
    for n, (dx, dc) in enumerate(LIB_PEERS):
        cp = pltpu.make_async_remote_copy(
            src_ref=req_ref,
            dst_ref=asked.at[mine],
            send_sem=table_sems.at[0, n],
            recv_sem=table_sems.at[1, n],
            device_id=device_of(lib_peer(me, dx, dc)),
            device_id_type=MESH,
        )
        cp.start()
        tables.append(cp)
    asked[mine] = req_ref[...]
    for cp in tables:
        cp.wait_recv()
    local = pltpu.make_async_copy(asked, asked_s, table_sems.at[0, 7])
    local.start()
    local.wait()
    loads[0].wait()
    own_box = (lax.div(mine, 4), lax.rem(mine, 4))
    waves = []
    for k in range(CAP):
        wave = []
        for n, (dx, dc) in enumerate(LIB_PEERS):
            cp = pltpu.make_async_remote_copy(
                src_ref=stage.at[n // 4, n % 4, k],
                dst_ref=slots.at[own_box[0], own_box[1], k],
                send_sem=tile_sems.at[0, n * CAP + k],
                recv_sem=tile_sems.at[1, n * CAP + k],
                device_id=device_of(lib_peer(me, dx, dc)),
                device_id_type=MESH,
            )
            wave.append(cp)
        waves.append(wave)

    def stage_tile(n, k):
        at = lib_peer(me, *LIB_PEERS[n])
        peer = at["x"] * 2 + at["c"]
        stage[n // 4, n % 4, k] = lib_ref[asked_s[peer, mine, k]]

    for n in range(len(LIB_PEERS)):
        stage_tile(n, 0)
        waves[0][n].start()
    for k in range(1, CAP):
        for n in range(len(LIB_PEERS)):
            stage_tile(n, k)
    for cp in loads[1:]:
        cp.start()
    for k in range(CAP):
        slots[own_box[0], own_box[1], k] = lib_ref[asked_s[mine, mine, k]]
    return tables, waves


def w_part(ref, j):
    return ref.at[pl.ds(2 * j, 2)]


def step_kernel(
    x_hbm, g_hbm, gain_ref, w_hbm, lib_hbm, wanted, home,
    out_hbm, grad_hbm, wsum_ref, gsum_ref,
    req_ref, order_ref, g_ref, w_ref, lib_ref, load_sems,
    inv_ref, q_ref, dm_ref, mixed_ref, dsh_ref, kvs, tt_ref, at_ref, stage, slots,
    asked, asked_s, table_sems, tile_sems, gslots, gsend, grecv, pair_sems, free_sem,
    store_sems, *piece_bufs,
):
    me = my_coords()
    pairs = [(lib_hbm, lib_ref), (x_hbm, dsh_ref), (w_part(w_hbm, 0), w_part(w_ref, 0)), (g_hbm, g_ref)]
    pairs += [(w_part(w_hbm, j), w_part(w_ref, j)) for j in (3, 1, 2)]
    loads = [pltpu.make_async_copy(a, b, load_sems.at[n]) for n, (a, b) in enumerate(pairs)]
    loads[0].start()

    barrier = pltpu.get_barrier_semaphore()
    peers = [lib_peer(me, dx, dc) for dx, dc in LIB_PEERS]
    peers += [{**me, a: along(me, a, s)} for a in ("y", "z") for s in (1, 2, 3)]
    for at in peers:
        pl.semaphore_signal(barrier, inc=1, device_id=device_of(at), device_id_type=MESH)
    req_ref[...] = request_table(wanted, home, order_ref)
    pl.semaphore_wait(barrier, len(peers))

    tables, waves = start_fetch(
        me, req_ref, lib_ref, loads, asked, asked_s, stage, slots, table_sems, tile_sems
    )

    def matrix(j):
        return w_part(w_ref, j)[...].reshape(D, D)

    for cp in loads[1:5]:
        cp.wait()

    @pl.loop(0, 2)
    def _(s):
        rows = pl.ds(pl.multiple_of(s * SEQ, SEQ), SEQ)
        x = dsh_ref[rows].astype(F32)
        inv = lax.rsqrt(jnp.mean(x * x, axis=1, keepdims=True) + EPSILON)
        inv_ref[rows] = inv
        normed = (x * inv * gain_ref[...]).astype(BF16)
        at_ref[0, :, rows] = normed.T
        q_ref[rows] = shift_up_rows(dot(normed, matrix(0))).astype(BF16)
        dm_ref[rows] = shift_up_rows(dot(g_ref[rows], matrix(3), ((1,), (1,)))).astype(BF16)

    for cp in loads[5:]:
        cp.wait()

    for k in range(CAP):
        for n in range(len(LIB_PEERS)):
            waves[k][n].wait_send()
            if k + 1 < CAP:
                waves[k + 1][n].start()
        for cp in waves[k]:
            cp.wait_recv()

        @pl.loop(0, 2)
        def _(h):
            t = slots[h, :, k].reshape(512, D)
            for half in range(2):
                c = slice(half * 512, half * 512 + 512)
                for m in range(2):
                    w = w_part(w_ref, 1 + m)[:, :, :, :, c].reshape(D, 512)
                    rows = dot(t, w).astype(BF16)
                    for o in range(4):
                        tile = rows[o * 128 : o * 128 + 128].reshape(4, 32, 512)
                        kvs[m, h * 16 + o * CAP + k, :, :, c] = tile

    pl.semaphore_signal(free_sem, inc=1, device_id=moved(me, "c", 1), device_id_type=MESH)

    @pl.loop(0, 16)
    def _(i):
        o = order_ref[i]
        t = slots[lax.div(o, 16), lax.rem(lax.div(o, 4), 4), lax.rem(o, 4)].reshape(128, D)
        tt_ref[:, pl.ds(pl.multiple_of(i * 128, 128), 128)] = t.T

    @pl.loop(0, 8)
    def _(b):
        attend(b, order_ref, q_ref, kvs.at[0], kvs.at[1], lib_ref, mixed_ref)

    @pl.loop(0, 2)
    def _(s):
        rows = pl.ds(pl.multiple_of(s * SEQ, SEQ), SEQ)
        attn = shift_down_rows(mixed_ref[rows].astype(F32)).astype(BF16)
        mixed_ref[rows] = attn
        at_ref[1, :, rows] = attn.T

    for cp in tables:
        cp.wait_send()

    def weight_terms(p):
        cols = slice(p * 256, p * 256 + 256)

        for j in range(4):
            for z in range(4):
                rows = slice(z * 256, z * 256 + 256)
                if j == 0:
                    res = dot(at_ref[0, rows, :], dsh_ref[:, cols])
                elif j == 3:
                    res = dot(at_ref[1, rows, :], g_ref[:, cols])
                else:
                    res = dot(tt_ref[rows, :], slots[j - 1, :, :, :, :, cols].reshape(2048, 256))
                res = res.astype(BF16)
                for xi in range(4):
                    for ci in range(2):
                        r0 = (xi * 2 + ci) * 32
                        stage[ci, j, z, xi, :, cols] = res[r0 : r0 + 32]

    def back(g):
        @pl.loop(0, 2)
        def _(b):
            attend_back(
                b * 4, 4, g, order_ref, q_ref, dm_ref, kvs.at[0], kvs.at[1], lib_ref, slots, dsh_ref
            )

        for s in range(2):
            at = (pl.ds(s * SEQ, SEQ), slice(g * 256, g * 256 + 256))
            dsh_ref[at] = shift_down_rows(dsh_ref[at].astype(F32)).astype(BF16)

    stores = []

    def store(src, dst, rows):
        n = len(stores)
        stores.append(pltpu.make_async_copy(src.at[rows], dst.at[rows], store_sems.at[n]))
        stores[n].start()

    def out_rows(s):
        rows = pl.ds(s * SEQ, SEQ)
        x = q_ref[rows].astype(F32)
        mixed_ref[rows] = (x + dot(mixed_ref[rows], matrix(3))).astype(BF16)
        store(mixed_ref, out_hbm, rows)

    def grad_rows(s):
        rows = pl.ds(s * SEQ, SEQ)
        x = q_ref[rows].astype(F32)
        inv = inv_ref[rows]
        dn = dot(dsh_ref[rows], matrix(0), ((1,), (1,)))
        dnx = dn * x * inv
        term = jnp.sum(dnx, axis=0, keepdims=True)
        gslots[0] = term if s == 0 else gslots[0] + term
        dh = dn * gain_ref[...]
        inner = jnp.mean(dh * x, axis=1, keepdims=True)
        dx = inv * dh - x * (inv * inv * inv) * inner
        dsh_ref[rows] = (g_ref[rows].astype(F32) + dx).astype(BF16)
        store(dsh_ref, grad_hbm, rows)

    sent = []
    paired = w_ref.at[pl.ds(2, 4)]
    n_each = len(piece_bufs) // (2 * PARTS)
    pair = {}
    flow = {}

    def send_part(p):
        if p == 0:
            pl.semaphore_wait(free_sem, 1)
        pair[p] = start_pair(me, p, stage, paired, pair_sems)
        sent.append(pair[p])

    def sum_part(p):
        end_pair(me, p, stage, paired, pair[p])
        flow[p] = []
        for h in range(2):
            q = 2 * p + h
            bufs = piece_bufs[q * n_each : (q + 1) * n_each]
            data = paired.at[:, :, :, :, pl.ds(q * 128, 128)]
            flow[p].append(reduce_piece(me, q, data, bufs, wsum_ref, sent))
            next(flow[p][-1])

    def advance(p):
        for f in flow[p]:
            next(f, None)

    back(0)
    weight_terms(0)
    send_part(0)
    back(1)
    sum_part(0)
    weight_terms(1)
    send_part(1)
    back(2)
    sum_part(1)
    advance(0)
    weight_terms(2)
    send_part(2)
    back(3)
    x_again = pltpu.make_async_copy(x_hbm, q_ref, load_sems.at[7])
    x_again.start()
    sum_part(2)
    advance(1)
    advance(0)
    weight_terms(3)
    send_part(3)
    x_again.wait()
    out_rows(0)
    sum_part(3)
    grad_rows(0)
    grad_rows(1)
    gain_flow = reduce_gain(me, gslots, gsend, grecv, sent)
    next(gain_flow)
    advance(2)
    advance(1)
    advance(0)
    out_rows(1)
    advance(3)
    next(gain_flow)
    advance(2)
    advance(1)
    advance(3)
    next(gain_flow)
    advance(2)
    advance(3)
    next(gain_flow, None)
    for cp in sent:
        cp.wait_send()
    for cp in stores:
        cp.wait()
    index = lax.axis_index("dp") * 8 + lax.axis_index("lib")
    gsum_ref[...] = pltpu.roll(gslots[0], lax.rem(D - index * 8, D), 1)[:, :128]


def train_step(hidden, cot, gains, weights, library, neighbours, tile_home):
    rows5 = (2, 4, 4, 4, 32, D)
    scratch = [
        pltpu.VMEM((8, 128), jnp.int32),
        pltpu.SMEM((16,), jnp.int32),
        pltpu.VMEM((512, D), BF16),
        pltpu.VMEM((8, 4, 4, 32, D), BF16),
        pltpu.VMEM((16, 4, 32, D), BF16),
        pltpu.SemaphoreType.DMA((8,)),
        pltpu.VMEM((512, 1), F32),
        pltpu.VMEM((512, D), BF16),
        pltpu.VMEM((512, D), BF16),
        pltpu.VMEM((512, D), BF16),
        pltpu.VMEM((512, D), BF16),
        pltpu.VMEM((2, 32, 4, 32, D), BF16),
        pltpu.VMEM((D, 2048), BF16),
        pltpu.VMEM((2, D, 512), BF16),
        pltpu.VMEM(rows5, BF16),
        pltpu.VMEM(rows5, BF16),
        pltpu.VMEM((8, 8, 128), jnp.int32),
        pltpu.SMEM((8, 8, 128), jnp.int32),
        pltpu.SemaphoreType.DMA((2, 8)),
        pltpu.SemaphoreType.DMA((2, 28)),
        pltpu.VMEM((17, 1, D), F32),
        pltpu.SemaphoreType.DMA((13,)),
        pltpu.SemaphoreType.DMA((13,)),
        pltpu.SemaphoreType.DMA((2, PARTS)),
        pltpu.SemaphoreType.REGULAR,
        pltpu.SemaphoreType.DMA((4,)),
    ]
    for _ in range(2 * PARTS):
        scratch += piece_scratch()
    hbm = pl.BlockSpec(memory_space=pl.ANY)
    smem = pl.BlockSpec(memory_space=pltpu.SMEM)
    vmem = pl.BlockSpec(memory_space=pltpu.VMEM)
    return pl.pallas_call(
        step_kernel,
        out_shape=(
            jax.ShapeDtypeStruct((512, D), BF16),
            jax.ShapeDtypeStruct((512, D), BF16),
            jax.ShapeDtypeStruct((32, D), F32),
            jax.ShapeDtypeStruct((1, 128), F32),
        ),
        in_specs=[hbm, hbm, vmem, hbm, hbm, smem, smem],
        out_specs=(hbm, hbm, vmem, vmem),
        scratch_shapes=scratch,
        compiler_params=pltpu.CompilerParams(
            collective_id=1, has_side_effects=True, vmem_limit_bytes=67000000
        ),
        name="train_step",
    )(hidden, cot, gains, weights.reshape(8, 4, 4, 32, D), library.reshape(16, 4, 32, D), neighbours, tile_home)


def hand_over_kernel(out_in, grad_in, w_in, g_in, out_ref, grad_ref, w_ref, g_ref, sems):
    copies = []
    for src, dst, n in ((out_in, out_ref, 4), (grad_in, grad_ref, 4), (w_in, w_ref, 1)):
        rows = src.shape[0] // n
        for k in range(n):
            part = pl.ds(k * rows, rows)
            copies.append(
                pltpu.make_async_copy(src.at[part], dst.at[part], sems.at[len(copies)])
            )
            copies[-1].start()
    g_ref[...] = g_in[0, :8]
    for cp in copies:
        cp.wait()


def hand_over(out, grad, w_share, g_sum):
    hbm = pl.BlockSpec(memory_space=pl.ANY)
    vmem = pl.BlockSpec(memory_space=pltpu.VMEM)
    return pl.pallas_call(
        hand_over_kernel,
        out_shape=(
            jax.ShapeDtypeStruct(out.shape, out.dtype),
            jax.ShapeDtypeStruct(grad.shape, grad.dtype),
            jax.ShapeDtypeStruct(w_share.shape, w_share.dtype),
            jax.ShapeDtypeStruct((8,), F32),
        ),
        in_specs=[vmem] * 4,
        out_specs=(hbm, hbm, hbm, vmem),
        scratch_shapes=[pltpu.SemaphoreType.DMA((9,))],
        name="hand_over",
    )(out, grad, w_share, g_sum)


def body(hidden_in, cotangent, gains, weights, library, neighbours, tile_home):
    results = train_step(
        hidden_in, cotangent, gains, weights[0], library, neighbours, tile_home
    )
    return hand_over(*results)


def solution(mesh):
    return jax.shard_map(
        body,
        mesh=mesh,
        in_specs=(
            P(("dp", "lib"), None),
            P(("dp", "lib"), None),
            P(),
            P(),
            P(("dp", "lib"), None, None),
            P(("dp", "lib"), None),
            P("dp", None),
        ),
        out_specs=(
            P(("dp", "lib"), None),
            P(("dp", "lib"), None),
            P(("dp", "lib"), None),
            P(("dp", "lib")),
        ),
        check_vma=False,
    )
```

time: 183 us -> 173 us (0.945)
  local copies, waits for them, and re-layouts: 8.1 us -> 1.35 us
  other arithmetic: 2.4 us -> 0 us
    unnamed x4 -> x1, local copies, waits for them, and re-layouts: 6.84 us -> 1.35 us
    pallas_call x1, Pallas kernels: 172 us -> 167 us  [train_step(): pl.pallas_call(step_kernel, out_shape=(jax.ShapeDtypeStruct((512, D), BF1...]
    pallas_call x0 -> x1, Pallas kernels: none -> 3.48 us  [hand_over(): pl.pallas_call(hand_over_kernel, out_shape=(jax.ShapeDtypeStruct(out.shap...]
where the time goes in v4:
time: 173 us
  Pallas kernels  171 us (99%)
    pallas_call x1, Pallas kernels, train_step(): pl.pallas_call(step_kernel, out_shape=(jax.ShapeDtypeStruct((512, D), BF1...  167 us
    pallas_call x1, Pallas kernels, hand_over(): pl.pallas_call(hand_over_kernel, out_shape=(jax.ShapeDtypeStruct(out.shap...  3.48 us

profile of v4, /device:TPU:0, one launch (start us, length us, event | category | flops | bytes accessed | tf_op | source)
XLA Modules:
  0.0 173.0 jit_solution(10037064143714912722)
XLA Ops:
  0.6 1.3 copy.11.wanted
  2.0 167.4 %train_step.1 = (bf16[512,1024]{1,0:T(8,128)(2,1)}, bf16[512,1024]{1,0:T(8,128)(2,1)}, f32[32,1024]{1,0:T(8,128)}, f32[1,128]{1,0:T(1,128)}) custom-call(bf16[512,1024]{1,0:T(8,128)(2,1)} %x_hbm.1, bf16[512,1024]{1,0:T(8,128)(2,1)} %g_hbm.1, f32[1,1024]{1,0:T(1,128)} %gain_ref.1, bf16[8,4,4,32,1024]{4,3,2,1,0:T(8,128)(2,1)} %bitcast.2, ...), custom_call_target="tpu_custom_call" | custom-call | tf_op jit(solution)/shard_map/train_step/pallas_call | solution.py:591
  169.3 3.5 %hand_over.1 = (bf16[512,1024]{1,0:T(8,128)(2,1)}, bf16[512,1024]{1,0:T(8,128)(2,1)}, f32[32,1024]{1,0:T(8,128)}, f32[8]{0:T(128)}) custom-call(bf16[512,1024]{1,0:T(8,128)(2,1)} %get-tuple-element.8.out_in, bf16[512,1024]{1,0:T(8,128)(2,1)} %get-tuple-element.9.grad_in, f32[32,1024]{1,0:T(8,128)} %get-tuple-element.10.w_in, f32[1,128]{1,0:T(1,128)} %get-tuple-element.11.g_in), custom_call_target="tpu_custom_call" | custom-call | tf_op jit(solution)/shard_map/hand_over/pallas_call | solution.py:627

commit v5 on v4

--- a/solution.py
+++ b/solution.py
@@ -69,13 +69,13 @@
     return shapes
 
 
-def start_pair(me, p, own, paired, sems):
+def start_pair(me, p, j, own, paired, sems):
     cols = slice(p * 256, p * 256 + 256)
     cp = pltpu.make_async_remote_copy(
-        src_ref=own.at[along(me, "c", 1), :, :, :, :, cols],
-        dst_ref=paired.at[:, :, :, :, cols],
-        send_sem=sems.at[0, p],
-        recv_sem=sems.at[1, p],
+        src_ref=own.at[along(me, "c", 1), j, :, :, :, cols],
+        dst_ref=paired.at[j, :, :, :, cols],
+        send_sem=sems.at[0, p * 4 + j],
+        recv_sem=sems.at[1, p * 4 + j],
         device_id=moved(me, "c", 1),
         device_id_type=MESH,
     )
@@ -83,17 +83,16 @@
     return cp
 
 
-def end_pair(me, p, own, paired, cp):
+def end_pair(me, p, own, paired, copies):
     cols = slice(p * 256, p * 256 + 256)
-    cp.wait_recv()
-
-    @pl.loop(0, 16)
-    def _(i):
-        yi = lax.div(i, 4)
-        zi = lax.rem(i, 4)
-        total = own[me["c"], yi, zi, :, :, cols].astype(F32)
-        total = total + paired[yi, zi, :, :, cols].astype(F32)
-        paired[yi, zi, :, :, cols] = total.astype(BF16)
+    for j, cp in copies:
+        cp.wait_recv()
+
+        @pl.loop(0, 4)
+        def _(z):
+            total = own[me["c"], j, z, :, :, cols].astype(F32)
+            total = total + paired[j, z, :, :, cols].astype(F32)
+            paired[j, z, :, :, cols] = total.astype(BF16)
 
 
 def reduce_piece(me, q, data, bufs, w_out, sent):
@@ -265,7 +264,7 @@
     table = jnp.zeros((8, 128), jnp.int32)
     owners = []
     for i in range(16):
-        stored = home[0, wanted[i // 2, i % 2]]
+        stored = home[0, wanted[i % 2, i // 2]]
         owner = lax.div(stored, 16)
         rank = jnp.int32(0)
         for before in owners:
@@ -273,24 +272,25 @@
         owners.append(owner)
         order[i] = owner * CAP + rank
         table = jnp.where((row == owner) & (col == rank), lax.rem(stored, 16), table)
-    return table
+    return table.reshape(8, 1, 128)
 
 
 def start_fetch(me, req_ref, lib_ref, loads, asked, asked_s, stage, slots, table_sems, tile_sems):
     mine = me["x"] * 2 + me["c"]
     tables = []
     for n, (dx, dc) in enumerate(LIB_PEERS):
+        at = lib_peer(me, dx, dc)
         cp = pltpu.make_async_remote_copy(
-            src_ref=req_ref,
+            src_ref=req_ref.at[at["x"] * 2 + at["c"]],
             dst_ref=asked.at[mine],
             send_sem=table_sems.at[0, n],
             recv_sem=table_sems.at[1, n],
-            device_id=device_of(lib_peer(me, dx, dc)),
+            device_id=device_of(at),
             device_id_type=MESH,
         )
         cp.start()
         tables.append(cp)
-    asked[mine] = req_ref[...]
+    asked[mine] = req_ref[mine]
     for cp in tables:
         cp.wait_recv()
     local = pltpu.make_async_copy(asked, asked_s, table_sems.at[0, 7])
@@ -316,7 +316,7 @@
     def stage_tile(n, k):
         at = lib_peer(me, *LIB_PEERS[n])
         peer = at["x"] * 2 + at["c"]
-        stage[n // 4, n % 4, k] = lib_ref[asked_s[peer, mine, k]]
+        stage[n // 4, n % 4, k] = lib_ref[asked_s[peer, 0, k]]
 
     for n in range(len(LIB_PEERS)):
         stage_tile(n, 0)
@@ -327,7 +327,7 @@
     for cp in loads[1:]:
         cp.start()
     for k in range(CAP):
-        slots[own_box[0], own_box[1], k] = lib_ref[asked_s[mine, mine, k]]
+        slots[own_box[0], own_box[1], k] = lib_ref[asked_s[mine, 0, k]]
     return tables, waves
 
 
@@ -386,12 +386,13 @@
             waves[k][n].wait_send()
             if k + 1 < CAP:
                 waves[k + 1][n].start()
-        for cp in waves[k]:
-            cp.wait_recv()
-
-        @pl.loop(0, 2)
-        def _(h):
-            t = slots[h, :, k].reshape(512, D)
+        for dx in (0, 1):
+            for n, (px, _) in enumerate(LIB_PEERS):
+                if px % 2 == dx:
+                    waves[k][n].wait_recv()
+            chips = [along(me, "x", dx), along(me, "x", dx + 2)]
+            t = [slots[lax.div(c, 2), pl.ds(lax.rem(c, 2) * 2, 2), k] for c in chips]
+            t = jnp.concatenate([a.reshape(256, D) for a in t], axis=0)
             for half in range(2):
                 c = slice(half * 512, half * 512 + 512)
                 for m in range(2):
@@ -399,7 +400,7 @@
                     rows = dot(t, w).astype(BF16)
                     for o in range(4):
                         tile = rows[o * 128 : o * 128 + 128].reshape(4, 32, 512)
-                        kvs[m, h * 16 + o * CAP + k, :, :, c] = tile
+                        kvs[m, (chips[o // 2] * 2 + o % 2) * CAP + k, :, :, c] = tile
 
     pl.semaphore_signal(free_sem, inc=1, device_id=moved(me, "c", 1), device_id_type=MESH)
 
@@ -409,7 +410,7 @@
         t = slots[lax.div(o, 16), lax.rem(lax.div(o, 4), 4), lax.rem(o, 4)].reshape(128, D)
         tt_ref[:, pl.ds(pl.multiple_of(i * 128, 128), 128)] = t.T
 
-    @pl.loop(0, 8)
+    @pl.loop(0, 8, unroll=2)
     def _(b):
         attend(b, order_ref, q_ref, kvs.at[0], kvs.at[1], lib_ref, mixed_ref)
 
@@ -423,10 +424,14 @@
     for cp in tables:
         cp.wait_send()
 
+    sent = []
+    pair = {}
+    paired = w_ref.at[pl.ds(2, 4)]
+
     def weight_terms(p):
         cols = slice(p * 256, p * 256 + 256)
-
-        for j in range(4):
+        pair[p] = []
+        for j in (1, 2, 0, 3):
             for z in range(4):
                 rows = slice(z * 256, z * 256 + 256)
                 if j == 0:
@@ -440,6 +445,11 @@
                     for ci in range(2):
                         r0 = (xi * 2 + ci) * 32
                         stage[ci, j, z, xi, :, cols] = res[r0 : r0 + 32]
+            if p == 0 and not pair[p]:
+                pl.semaphore_wait(free_sem, 1)
+            cp = start_pair(me, p, j, stage, paired, pair_sems)
+            sent.append(cp)
+            pair[p].append((j, cp))
 
     def back(g):
         @pl.loop(0, 2)
@@ -479,17 +489,8 @@
         dsh_ref[rows] = (g_ref[rows].astype(F32) + dx).astype(BF16)
         store(dsh_ref, grad_hbm, rows)
 
-    sent = []
-    paired = w_ref.at[pl.ds(2, 4)]
     n_each = len(piece_bufs) // (2 * PARTS)
-    pair = {}
     flow = {}
-
-    def send_part(p):
-        if p == 0:
-            pl.semaphore_wait(free_sem, 1)
-        pair[p] = start_pair(me, p, stage, paired, pair_sems)
-        sent.append(pair[p])
 
     def sum_part(p):
         end_pair(me, p, stage, paired, pair[p])
@@ -507,16 +508,13 @@
 
     back(0)
     weight_terms(0)
-    send_part(0)
     back(1)
     sum_part(0)
     weight_terms(1)
-    send_part(1)
     back(2)
     sum_part(1)
     advance(0)
     weight_terms(2)
-    send_part(2)
     back(3)
     x_again = pltpu.make_async_copy(x_hbm, q_ref, load_sems.at[7])
     x_again.start()
@@ -524,7 +522,6 @@
     advance(1)
     advance(0)
     weight_terms(3)
-    send_part(3)
     x_again.wait()
     out_rows(0)
     sum_part(3)
@@ -556,7 +553,7 @@
 def train_step(hidden, cot, gains, weights, library, neighbours, tile_home):
     rows5 = (2, 4, 4, 4, 32, D)
     scratch = [
-        pltpu.VMEM((8, 128), jnp.int32),
+        pltpu.VMEM((8, 1, 128), jnp.int32),
         pltpu.SMEM((16,), jnp.int32),
         pltpu.VMEM((512, D), BF16),
         pltpu.VMEM((8, 4, 4, 32, D), BF16),
@@ -572,14 +569,14 @@
         pltpu.VMEM((2, D, 512), BF16),
         pltpu.VMEM(rows5, BF16),
         pltpu.VMEM(rows5, BF16),
-        pltpu.VMEM((8, 8, 128), jnp.int32),
-        pltpu.SMEM((8, 8, 128), jnp.int32),
+        pltpu.VMEM((8, 1, 128), jnp.int32),
+        pltpu.SMEM((8, 1, 128), jnp.int32),
         pltpu.SemaphoreType.DMA((2, 8)),
         pltpu.SemaphoreType.DMA((2, 28)),
         pltpu.VMEM((17, 1, D), F32),
         pltpu.SemaphoreType.DMA((13,)),
         pltpu.SemaphoreType.DMA((13,)),
-        pltpu.SemaphoreType.DMA((2, PARTS)),
+        pltpu.SemaphoreType.DMA((2, 4 * PARTS)),
         pltpu.SemaphoreType.REGULAR,
         pltpu.SemaphoreType.DMA((4,)),
     ]
@@ -603,7 +600,7 @@
             collective_id=1, has_side_effects=True, vmem_limit_bytes=67000000
         ),
         name="train_step",
-    )(hidden, cot, gains, weights.reshape(8, 4, 4, 32, D), library.reshape(16, 4, 32, D), neighbours, tile_home)
+    )(hidden, cot, gains, weights.reshape(8, 4, 4, 32, D), library.reshape(16, 4, 32, D), neighbours.T, tile_home)
 
 
 def hand_over_kernel(out_in, grad_in, w_in, g_in, out_ref, grad_ref, w_ref, g_ref, sems):

time: 173 us -> 169 us (0.977)
  Pallas kernels: 171 us -> 168 us
    pallas_call x1, Pallas kernels: 167 us -> 164 us  [train_step(): pl.pallas_call(step_kernel, out_shape=(jax.ShapeDtypeStruct((512, D), BF1...]
where the time goes in v5:
time: 169 us; the launch traced here: 168 us
  Pallas kernels  168 us (99%)
    pallas_call x1, Pallas kernels, train_step(): pl.pallas_call(step_kernel, out_shape=(jax.ShapeDtypeStruct((512, D), BF1...  164 us
    pallas_call x1, Pallas kernels, hand_over(): pl.pallas_call(hand_over_kernel, out_shape=(jax.ShapeDtypeStruct(out.shap...  3.48 us

profile of v5, /device:TPU:0, one launch (start us, length us, event | category | flops | bytes accessed | tf_op | source)
XLA Modules:
  0.0 168.4 jit_solution(16196275431072326835)
XLA Ops:
  0.6 164.1 %train_step.1 = (bf16[512,1024]{1,0:T(8,128)(2,1)}, bf16[512,1024]{1,0:T(8,128)(2,1)}, f32[32,1024]{1,0:T(8,128)}, f32[1,128]{1,0:T(1,128)}) custom-call(bf16[512,1024]{1,0:T(8,128)(2,1)} %x_hbm.1, bf16[512,1024]{1,0:T(8,128)(2,1)} %g_hbm.1, f32[1,1024]{1,0:T(1,128)} %gain_ref.1, bf16[8,4,4,32,1024]{4,3,2,1,0:T(8,128)(2,1)} %bitcast.3, ...), custom_call_target="tpu_custom_call" | custom-call | tf_op jit(solution)/shard_map/train_step/pallas_call | solution.py:588
  164.7 3.5 %hand_over.1 = (bf16[512,1024]{1,0:T(8,128)(2,1)}, bf16[512,1024]{1,0:T(8,128)(2,1)}, f32[32,1024]{1,0:T(8,128)}, f32[8]{0:T(128)}) custom-call(bf16[512,1024]{1,0:T(8,128)(2,1)} %get-tuple-element.8.out_in, bf16[512,1024]{1,0:T(8,128)(2,1)} %get-tuple-element.9.grad_in, f32[32,1024]{1,0:T(8,128)} %get-tuple-element.10.w_in, f32[1,128]{1,0:T(1,128)} %get-tuple-element.11.g_in), custom_call_target="tpu_custom_call" | custom-call | tf_op jit(solution)/shard_map/hand_over/pallas_call | solution.py:624

commit v6 on v5

--- a/solution.py
+++ b/solution.py
@@ -450,6 +450,8 @@
             cp = start_pair(me, p, j, stage, paired, pair_sems)
             sent.append(cp)
             pair[p].append((j, cp))
+            if p == PARTS - 1 and len(pair[p]) > 1:
+                end_pair(me, p, stage, paired, pair[p][-2:-1])
 
     def back(g):
         @pl.loop(0, 2)
@@ -493,7 +495,7 @@
     flow = {}
 
     def sum_part(p):
-        end_pair(me, p, stage, paired, pair[p])
+        end_pair(me, p, stage, paired, pair[p][-1:] if p == PARTS - 1 else pair[p])
         flow[p] = []
         for h in range(2):
             q = 2 * p + h

time: 169 us -> 169 us (level)
  no operation moved by 1% of the time
where the time goes in v6:
time: 169 us
  Pallas kernels  168 us (99%)
    pallas_call x1, Pallas kernels, train_step(): pl.pallas_call(step_kernel, out_shape=(jax.ShapeDtypeStruct((512, D), BF1...  165 us
    pallas_call x1, Pallas kernels, hand_over(): pl.pallas_call(hand_over_kernel, out_shape=(jax.ShapeDtypeStruct(out.shap...  3.48 us

profile of v6, /device:TPU:0, one launch (start us, length us, event | category | flops | bytes accessed | tf_op | source)
XLA Modules:
  0.0 168.9 jit_solution(8719970426443055158)
XLA Ops:
  0.6 164.6 %train_step.1 = (bf16[512,1024]{1,0:T(8,128)(2,1)}, bf16[512,1024]{1,0:T(8,128)(2,1)}, f32[32,1024]{1,0:T(8,128)}, f32[1,128]{1,0:T(1,128)}) custom-call(bf16[512,1024]{1,0:T(8,128)(2,1)} %x_hbm.1, bf16[512,1024]{1,0:T(8,128)(2,1)} %g_hbm.1, f32[1,1024]{1,0:T(1,128)} %gain_ref.1, bf16[8,4,4,32,1024]{4,3,2,1,0:T(8,128)(2,1)} %bitcast.3, ...), custom_call_target="tpu_custom_call" | custom-call | tf_op jit(solution)/shard_map/train_step/pallas_call | solution.py:590
  165.2 3.5 %hand_over.1 = (bf16[512,1024]{1,0:T(8,128)(2,1)}, bf16[512,1024]{1,0:T(8,128)(2,1)}, f32[32,1024]{1,0:T(8,128)}, f32[8]{0:T(128)}) custom-call(bf16[512,1024]{1,0:T(8,128)(2,1)} %get-tuple-element.8.out_in, bf16[512,1024]{1,0:T(8,128)(2,1)} %get-tuple-element.9.grad_in, f32[32,1024]{1,0:T(8,128)} %get-tuple-element.10.w_in, f32[1,128]{1,0:T(1,128)} %get-tuple-element.11.g_in), custom_call_target="tpu_custom_call" | custom-call | tf_op jit(solution)/shard_map/hand_over/pallas_call | solution.py:626
